TPU v7x, 128 devices: a whole 4x4x4 slice. The times are simulated.
128 devices in a mesh: member: 2 (over y_hi), tile: 64 (over z, y_lo, x, core).
Axes of the slice: x: 4, y: 4 (y_hi: 2, y_lo: 2; y = y_hi * 2 + y_lo), z: 4, core: 2. Of those that a mesh axis runs over, the one named last changes fastest.
Arguments:
- vectors: float32 [4, 3, 8, 2048, 512], P('member', None, None, 'tile'), may hold values from -6 to 6
- trajectory: bfloat16 [4, 3, 8, 2048, 512], P('member', None, None, 'tile'), may hold values from -1 to 1
- slot_table: int32 [4], replicated, may hold values from 0 to 3, each once
Outputs:
- advanced: float32 [4, 3, 8, 2048, 512], P('member', None, None, 'tile')
Inputs may be any that keep to these rules, and one draw needn't show every extreme that they name: `slot_table`: each slot appears once; slot g lies on member index g // 2.
All inputs are finite; a program needn't handle non-finite values.
Results may differ from a plain program's by a relative error of at most 0.0003.
Values may be sent and summed in bfloat16 or wider, within the bound.
No kernel may reach another device: no remote copies, remote signals or barrier semaphores. Data moves between devices by JAX's collectives and lax.ppermute only.
A program may use at most 128 MiB of HBM per device.

v0:
```python
import functools

import jax
import jax.numpy as jnp
import numpy as np
from jax import lax
from jax.experimental import pallas as pl
from jax.experimental.pallas import tpu as pltpu
from jax.sharding import PartitionSpec as P

STEPS = 4
COURANT = 0.8
NK, LANES, LEV, LON, NLAT = 4, 128, 8, 32, 512
CORE = LON * LEV
WIDE = 6
RIM = WIDE * LEV
NEAR = 2 * LEV
EXT = CORE + 2 * RIM
VMEM_LIMIT = 48 * 1024 * 1024
F32, BF16 = jnp.float32, jnp.bfloat16


def lane_order():
    order = np.zeros((NLAT, NLAT), np.float32)
    for lat in range(NLAT):
        order[lat, (lat % NK) * LANES + lat // NK] = 1.0
    return order


def dot(a, b):
    return jnp.dot(a, b, preferred_element_type=F32)


def split_dot(x, order):
    high = x.astype(BF16)
    rest = (x - high.astype(F32)).astype(BF16)
    return dot(high, order) + dot(rest, order)


def scatter_rows(y, dst):
    for lev in range(LEV):
        for tile in range(LON // 8):
            for k in range(NK):
                dst[k, pl.ds(tile * 64 + lev, 8, stride=LEV), :] = y[
                    lev * LON + tile * 8 : lev * LON + tile * 8 + 8, k * LANES : (k + 1) * LANES
                ]


def gather_rows(src):
    rows = []
    for lev in range(LEV):
        for tile in range(LON // 8):
            rows.append(
                jnp.concatenate([src[k, pl.ds(tile * 64 + lev, 8, stride=LEV), :] for k in range(NK)], axis=1)
            )
    return jnp.concatenate(rows, axis=0)


def pack_edges(p, head_ref, tail_ref, at):
    for k in range(NK):
        head = p[k, pl.ds(0, RIM), :]
        tail = p[k, pl.ds(CORE - RIM, RIM), :]
        high, last = head.astype(BF16), tail.astype(BF16)
        head_ref[(*at, k, pl.ds(0, RIM), slice(None))] = high
        head_ref[(*at, k, pl.ds(RIM, NEAR), slice(None))] = (head[:NEAR] - high[:NEAR].astype(F32)).astype(BF16)
        tail_ref[(*at, k, pl.ds(0, RIM), slice(None))] = last
        tail_ref[(*at, k, pl.ds(RIM, NEAR), slice(None))] = (tail[RIM - NEAR :] - last[RIM - NEAR :].astype(F32)).astype(BF16)


def base_kernel(slot_ref, traj_ref, order_ref, core_ref, head_ref, tail_ref, rows):
    y = dot(traj_ref[0, 0].reshape(LEV * LON, NLAT), order_ref[...])
    scatter_rows(y, rows)
    for k in range(NK):
        core_ref[0, k] = rows[k].astype(BF16)
        head_ref[0, k] = rows[k, pl.ds(0, RIM), :].astype(BF16)
        tail_ref[0, k] = rows[k, pl.ds(CORE - RIM, RIM), :].astype(BF16)


def convert_base(slot, trajectory, order):
    spec = pltpu.PrefetchScalarGridSpec(
        num_scalar_prefetch=1,
        grid=(3,),
        in_specs=[
            pl.BlockSpec((1, 1, LEV, LON, NLAT), lambda c, slot: (slot[0], c, 0, 0, 0)),
            pl.BlockSpec((NLAT, NLAT), lambda c, slot: (0, 0)),
        ],
        out_specs=[
            pl.BlockSpec((1, NK, CORE, LANES), lambda c, slot: (c, 0, 0, 0)),
            pl.BlockSpec((1, NK, RIM, LANES), lambda c, slot: (c, 0, 0, 0)),
            pl.BlockSpec((1, NK, RIM, LANES), lambda c, slot: (c, 0, 0, 0)),
        ],
        scratch_shapes=[pltpu.VMEM((NK, CORE, LANES), F32)],
    )
    return pl.pallas_call(
        base_kernel,
        grid_spec=spec,
        out_shape=[
            jax.ShapeDtypeStruct((3, NK, CORE, LANES), BF16),
            jax.ShapeDtypeStruct((3, NK, RIM, LANES), BF16),
            jax.ShapeDtypeStruct((3, NK, RIM, LANES), BF16),
        ],
        compiler_params=pltpu.CompilerParams(vmem_limit_bytes=VMEM_LIMIT),
        cost_estimate=pl.CostEstimate(flops=4_000_000_000, bytes_accessed=2_000_000, transcendentals=0),
        name="convert_base",
    )(slot, trajectory, order)


def vectors_kernel(vec_ref, order_ref, core_ref, head_ref, tail_ref):
    y = split_dot(vec_ref[0, 0].reshape(LEV * LON, NLAT), order_ref[...])
    scatter_rows(y, core_ref.at[0, 0])
    pack_edges(core_ref.at[0, 0], head_ref, tail_ref, (0, 0))


def convert_vectors(vectors, order):
    nv = vectors.shape[0]
    return pl.pallas_call(
        vectors_kernel,
        grid=(nv, 3),
        in_specs=[
            pl.BlockSpec((1, 1, LEV, LON, NLAT), lambda v, c: (v, c, 0, 0, 0)),
            pl.BlockSpec((NLAT, NLAT), lambda v, c: (0, 0)),
        ],
        out_specs=[
            pl.BlockSpec((1, 1, NK, CORE, LANES), lambda v, c: (v, c, 0, 0, 0)),
            pl.BlockSpec((1, 1, NK, RIM + NEAR, LANES), lambda v, c: (v, c, 0, 0, 0)),
            pl.BlockSpec((1, 1, NK, RIM + NEAR, LANES), lambda v, c: (v, c, 0, 0, 0)),
        ],
        out_shape=[
            jax.ShapeDtypeStruct((nv, 3, NK, CORE, LANES), F32),
            jax.ShapeDtypeStruct((nv, 3, NK, RIM + NEAR, LANES), BF16),
            jax.ShapeDtypeStruct((nv, 3, NK, RIM + NEAR, LANES), BF16),
        ],
        compiler_params=pltpu.CompilerParams(vmem_limit_bytes=VMEM_LIMIT),
        cost_estimate=pl.CostEstimate(flops=4_000_000_000, bytes_accessed=7_000_000, transcendentals=0),
        name="convert_vectors",
    )(vectors, order)


def lat_difference(v, masks):
    first, last = masks
    below = jnp.where(first, 0.0, pltpu.roll(v[3], 1, axis=1))
    above = jnp.where(last, 0.0, pltpu.roll(v[0], LANES - 1, axis=1))
    return [v[1] - below, v[2] - v[0], v[3] - v[1], above - v[2]]


def lane_masks():
    lane = lax.broadcasted_iota(jnp.int32, (8, LANES), 1)
    return lane == 0, lane == LANES - 1


def derive(base, der, row, count):
    masks = lane_masks()
    for c in range(3):
        win = [[base[c, k, pl.ds(row + 8 * i - 16, 8), :] for k in range(NK)] for i in range(count + 4)]
        for i in range(count):
            at = pl.ds(row + 8 * i, 8)
            diff = lat_difference(win[i + 2], masks)
            for k in range(NK):
                dx = (8.0 * (win[i + 3][k] - win[i + 1][k]) - (win[i + 4][k] - win[i][k])) * (-COURANT / 12.0)
                dy = diff[k] * (-COURANT / 2.0)
                der[2 + c, k, at, :] = dx + 1.0 if c == 0 else dx
                der[5 + c, k, at, :] = dy + 1.0 if c == 1 else dy
                if c == 0:
                    der[0, k, at, :] = win[i + 2][k] * (-COURANT / 12.0)
                if c == 1:
                    der[1, k, at, :] = win[i + 2][k] * (-COURANT / 2.0)


def stage(src, start, der, row, count, keep, scale, put):
    masks = lane_masks()
    mid = [[[src[c, k, pl.ds(row + 8 * i, 8), :] for k in range(NK)] for i in range(count)] for c in range(2)]
    for c in range(3):
        win = [[src[c, k, pl.ds(row + 8 * i - 16, 8), :] for k in range(NK)] for i in range(count + 4)]
        for i in range(count):
            at = pl.ds(row + 8 * i, 8)
            diff = lat_difference(win[i + 2], masks)
            for k in range(NK):
                dx = 8.0 * (win[i + 3][k] - win[i + 1][k]) - (win[i + 4][k] - win[i][k])
                s = der[0, k, at, :] * dx + der[1, k, at, :] * diff[k]
                s = s + mid[0][i][k] * der[2 + c, k, at, :] + mid[1][i][k] * der[5 + c, k, at, :]
                if c == 2:
                    s = s + win[i + 2][k]
                if keep:
                    s = s + keep * start[c, k, at, :]
                if scale != 1.0:
                    s = s * scale
                put(c, k, row + 8 * i, s)


def sweep(low, high, count, body):
    rows = count * LEV

    def at(i, carry):
        body(pl.multiple_of(low + i * rows, LEV))
        return carry

    lax.fori_loop(0, (high - low) // rows, at, 0)


def step_kernel(choices, last, *refs):
    which_ref, p_ref, left_ref, right_ref = refs[:4]
    sets = [refs[4 + 3 * i : 7 + 3 * i] for i in range(len(choices))]
    rest = refs[4 + 3 * len(choices) :]
    if last:
        order_ref, out_ref, fetched, base, der, one, two, three, sems = rest
    else:
        out_ref, head_ref, tail_ref, fetched, base, der, one, two, three, sems = rest

    def copies(group):
        core, left, right = group
        return [
            pltpu.make_async_copy(left, fetched.at[:, :, pl.ds(0, RIM), :], sems.at[0]),
            pltpu.make_async_copy(core, fetched.at[:, :, pl.ds(RIM, CORE), :], sems.at[1]),
            pltpu.make_async_copy(right, fetched.at[:, :, pl.ds(RIM + CORE, RIM), :], sems.at[2]),
        ]

    v = pl.program_id(0)

    @pl.when(v == 0)
    def _():
        for choice, group in zip(choices, sets):

            @pl.when(which_ref[0] == choice)
            def _(group=group):
                for copy in copies(group):
                    copy.start()
                for copy in copies(group):
                    copy.wait()

        for c in range(3):
            for k in range(NK):
                base[c, k] = fetched[c, k].astype(F32)
        sweep(2 * LEV, EXT - 2 * LEV, 2, lambda row: derive(base, der, row, 2))

    for c in range(3):
        for k in range(NK):
            one[c, k, pl.ds(RIM, CORE), :] = p_ref[0, c, k]
            far = left_ref[0, c, k, pl.ds(0, RIM), :].astype(F32)
            near = left_ref[0, c, k, pl.ds(RIM, NEAR), :].astype(F32)
            one[c, k, pl.ds(0, RIM - NEAR), :] = far[: RIM - NEAR]
            one[c, k, pl.ds(RIM - NEAR, NEAR), :] = far[RIM - NEAR :] + near
            far = right_ref[0, c, k, pl.ds(0, RIM), :].astype(F32)
            near = right_ref[0, c, k, pl.ds(RIM, NEAR), :].astype(F32)
            one[c, k, pl.ds(RIM + CORE, NEAR), :] = far[:NEAR] + near
            one[c, k, pl.ds(RIM + CORE + NEAR, RIM - NEAR), :] = far[NEAR:]

    def into(ref, shift=0):
        def put(c, k, row, s):
            ref[c, k, pl.ds(row - shift, LEV), :] = s

        return put

    final = three if last else out_ref.at[0]
    sweep(2 * LEV, EXT - 2 * LEV, 2, lambda row: stage(one, one, der, row, 2, 0.0, 1.0, into(two)))
    sweep(4 * LEV, EXT - 4 * LEV, 2, lambda row: stage(two, one, der, row, 2, 3.0, 1.0, into(three)))
    if last:
        final = two
    sweep(
        6 * LEV,
        EXT - 6 * LEV,
        2,
        lambda row: stage(three, one, der, row, 2, 2.0, 1.0 / 6.0, into(final, RIM)),
    )
    if last:
        for c in range(3):
            out_ref[0, c] = split_dot(gather_rows(two.at[c]), order_ref[...]).reshape(LEV, LON, NLAT)
    else:
        for c in range(3):
            pack_edges(out_ref.at[0, c], head_ref, tail_ref, (0, c))


def advance(which, pert, edges, choices, groups, order, last):
    nv = pert.shape[0]
    anywhere = pl.BlockSpec(memory_space=pl.ANY)
    edge = pl.BlockSpec((1, 3, NK, RIM + NEAR, LANES), lambda v: (v, 0, 0, 0, 0))
    field = pl.BlockSpec((1, 3, NK, CORE, LANES), lambda v: (v, 0, 0, 0, 0))
    in_specs = [pl.BlockSpec(memory_space=pltpu.SMEM), field, edge, edge] + [anywhere] * (3 * len(groups))
    args = [which, pert, *edges] + [part for group in groups for part in group]
    if last:
        in_specs.append(pl.BlockSpec((NLAT, NLAT), lambda v: (0, 0)))
        args.append(order)
        out_specs = pl.BlockSpec((1, 3, LEV, LON, NLAT), lambda v: (v, 0, 0, 0, 0))
        out_shape = jax.ShapeDtypeStruct((nv, 3, LEV, LON, NLAT), F32)
    else:
        out_specs = [field, edge, edge]
        out_shape = [
            jax.ShapeDtypeStruct((nv, 3, NK, CORE, LANES), F32),
            jax.ShapeDtypeStruct((nv, 3, NK, RIM + NEAR, LANES), BF16),
            jax.ShapeDtypeStruct((nv, 3, NK, RIM + NEAR, LANES), BF16),
        ]
    return pl.pallas_call(
        functools.partial(step_kernel, choices, last),
        grid=(nv,),
        in_specs=in_specs,
        out_specs=out_specs,
        out_shape=out_shape,
        scratch_shapes=[
            pltpu.VMEM((3, NK, EXT, LANES), BF16),
            pltpu.VMEM((3, NK, EXT, LANES), F32),
            pltpu.VMEM((8, NK, EXT, LANES), F32),
        ]
        + [pltpu.VMEM((3, NK, EXT, LANES), F32)] * 3
        + [pltpu.SemaphoreType.DMA((3,))],
        compiler_params=pltpu.CompilerParams(vmem_limit_bytes=VMEM_LIMIT),
        cost_estimate=pl.CostEstimate(flops=9_000_000_000, bytes_accessed=9_000_000, transcendentals=0),
        name="last_step" if last else "step",
    )(*args)


def neighbours(head, tail):
    count = lax.axis_size("tile")
    left = lax.ppermute(tail, "tile", [(i, (i + 1) % count) for i in range(count)])
    right = lax.ppermute(head, "tile", [((i + 1) % count, i) for i in range(count)])
    return left, right


def on_device(order, order_back, vectors, trajectory, slot_table):
    slots = trajectory.shape[0]
    me = lax.axis_index("member")
    owner = slot_table // slots
    local = slot_table % slots
    mine = owner == me
    first = jnp.where(mine[0], local[0], jnp.where(mine[1], local[1], local[2]))
    ranks = [sum((owner[e] == owner[s]).astype(jnp.int32) for e in range(s)) if s else jnp.int32(0) for s in range(STEPS)]
    which = [jnp.where(mine[s], ranks[s], 2 + ranks[s]).reshape(1) for s in range(STEPS)]

    swap = [(0, 1), (1, 0)]
    own, got = [], []
    for turn in range(2):
        slot = jnp.where(turn == 0, first, 1 - first).reshape(1)
        core, head, tail = convert_base(slot, trajectory, order)
        got.append(lax.ppermute(core, "member", swap))
        own.append((core, head, tail))
    own = [(core, *neighbours(head, tail)) for core, head, tail in own]
    got = [(core, *neighbours(core[:, :, :RIM], core[:, :, CORE - RIM :])) for core in got]
    groups = {0: own[0], 1: own[1], 2: got[0], 3: got[1]}

    pert, head, tail = convert_vectors(vectors, order)
    for s in range(STEPS):
        edges = neighbours(head, tail)
        choices = (0, 2) if s == 0 else (1, 3) if s == STEPS - 1 else (0, 1, 2, 3)
        last = s == STEPS - 1
        done = advance(which[s], pert, edges, choices, [groups[i] for i in choices], order_back, last)
        if last:
            return done
        pert, head, tail = done


def solution(mesh):
    order = lane_order()

    def program(vectors, trajectory, slot_table):
        body = functools.partial(on_device, jnp.asarray(order, BF16), jnp.asarray(order.T, BF16))
        spec = P("member", None, None, "tile", None)
        return jax.shard_map(body, mesh=mesh, in_specs=(spec, spec, P()), out_specs=spec, check_vma=False)(
            vectors, trajectory, slot_table
        )

    return program
```

profile of v0, /device:TPU:0, one launch (start us, length us, event | category | flops | bytes accessed | tf_op | source)
XLA Modules:
  0.0 168.2 jit_solution(7958576364981350771)
XLA Ops:
  5.8 1.4 copy-done
  7.2 1.0 copy-done.14
  8.2 2.0 %convert_base.2 = (bf16[3,4,256,128]{3,2,1,0:T(8,128)(2,1)S(1)}, bf16[3,4,48,128]{3,2,1,0:T(8,128)(2,1)}, bf16[3,4,48,128]{3,2,1,0:T(8,128)(2,1)}) custom-call(s32[1]{0:T(128)} %bitcast.14.slot_ref, bf16[2,3,8,32,512]{4,3,2,1,0:T(8,128)(2,1)S(1)} %copy-done, bf16[512,512]{1,0:T(8,128)(2,1)S(1)} %copy-done.14), custom_call_target="tpu_custom_call" | custom-call | flops 4000000000 | bytes 2000000 | tf_op jit(solution)/shard_map/convert_base/pallas_call | solution.py:94
  10.3 3.3 %collective-permute-start.4 = (bf16[3,4,256,128]{3,2,1,0:T(8,128)(2,1)S(1)}, bf16[3,4,256,128]{3,2,1,0:T(8,128)(2,1)S(1)}, u32[]{:S(2)}, u32[]{:S(2)}) collective-permute-start(bf16[3,4,256,128]{3,2,1,0:T(8,128)(2,1)S(1)} %get-tuple-element.26.refs_4_), channel_id=1, source_target_pairs={{0,64},{64,0},{1,65},{65,1},{2,66},{66,2},{3,67},{67,3},{4,68},{68... | collective-permute-start | bytes 2359304 | tf_op jit(solution)/shard_map/ppermute | solution.py:332
  13.5 6.2 %convert_vectors.1 = (f32[2,3,4,256,128]{4,3,2,1,0:T(8,128)S(1)}, bf16[2,3,4,64,128]{4,3,2,1,0:T(8,128)(2,1)}, bf16[2,3,4,64,128]{4,3,2,1,0:T(8,128)(2,1)}) custom-call(f32[2,3,8,32,512]{4,3,2,1,0:T(8,128)} %vec_ref.1, bf16[512,512]{1,0:T(8,128)(2,1)S(1)} %copy-done.14), custom_call_target="tpu_custom_call" | custom-call | flops 4000000000 | bytes 7000000 | tf_op jit(solution)/shard_map/convert_vectors/pallas_call | solution.py:116
  19.7 1.7 copy-done.16
  21.4 6.0 %collective-permute-start.1 = (bf16[2,3,4,64,128]{4,3,2,1,0:T(8,128)(2,1)}, bf16[2,3,4,64,128]{4,3,2,1,0:T(8,128)(2,1)}, u32[]{:S(2)}, u32[]{:S(2)}) collective-permute-start(bf16[2,3,4,64,128]{4,3,2,1,0:T(8,128)(2,1)} %get-tuple-element.25), channel_id=1, source_target_pairs={{1,0},{2,1},{3,2},{4,3},{5,4},{6,5},{7,6},{8,7},{9,8},{10,9},{11,1... | collective-permute-start | bytes 1179656 | tf_op jit(solution)/shard_map/ppermute | solution.py:313
  27.3 6.0 %collective-permute-start.3 = (bf16[3,4,48,128]{3,2,1,0:T(8,128)(2,1)}, bf16[3,4,48,128]{3,2,1,0:T(8,128)(2,1)}, u32[]{:S(2)}, u32[]{:S(2)}) collective-permute-start(bf16[3,4,48,128]{3,2,1,0:T(8,128)(2,1)} %get-tuple-element.28), channel_id=1, source_target_pairs={{1,0},{2,1},{3,2},{4,3},{5,4},{6,5},{7,6},{8,7},{9,8},{10,9},{11,1... | collective-permute-start | bytes 442376 | tf_op jit(solution)/shard_map/ppermute | solution.py:313
  33.3 3.6 %collective-permute-done.4.refs_7_.refs_10_ = bf16[3,4,256,128]{3,2,1,0:T(8,128)(2,1)S(1)} collective-permute-done((bf16[3,4,256,128]{3,2,1,0:T(8,128)(2,1)S(1)}, bf16[3,4,256,128]{3,2,1,0:T(8,128)(2,1)S(1)}, u32[]{:S(2)}, u32[]{:S(2)}) %collective-permute-start.4) | collective-permute-done | bytes 786464 | tf_op jit(solution)/shard_map/ppermute | solution.py:332
  37.6 6.0 %collective-permute-start.6 = (bf16[3,4,48,128]{3,2,1,0:T(8,128)(2,1)}, bf16[3,4,48,128]{3,2,1,0:T(8,128)(2,1)}, u32[]{:S(2)}, u32[]{:S(2)}) collective-permute-start(bf16[3,4,48,128]{3,2,1,0:T(8,128)(2,1)} %get-tuple-element.45), channel_id=1, source_target_pairs={{1,0},{2,1},{3,2},{4,3},{5,4},{6,5},{7,6},{8,7},{9,8},{10,9},{11,1... | collective-permute-start | bytes 442376 | tf_op jit(solution)/shard_map/ppermute | solution.py:313
  43.6 1.0 copy-done.15
  44.6 2.0 %convert_base.3 = (bf16[3,4,256,128]{3,2,1,0:T(8,128)(2,1)S(1)}, bf16[3,4,48,128]{3,2,1,0:T(8,128)(2,1)}, bf16[3,4,48,128]{3,2,1,0:T(8,128)(2,1)S(1)}) custom-call(s32[1]{0:T(128)} %bitcast.15.slot_ref, bf16[2,3,8,32,512]{4,3,2,1,0:T(8,128)(2,1)S(1)} %copy-done.1, bf16[512,512]{1,0:T(8,128)(2,1)S(1)} %copy-done.15), custom_call_target="tpu_custom_call" | custom-call | flops 4000000000 | bytes 2000000 | tf_op jit(solution)/shard_map/convert_base/pallas_call | solution.py:94
  47.8 3.3 %collective-permute-start.11 = (bf16[3,4,256,128]{3,2,1,0:T(8,128)(2,1)S(1)}, bf16[3,4,256,128]{3,2,1,0:T(8,128)(2,1)S(1)}, u32[]{:S(2)}, u32[]{:S(2)}) collective-permute-start(bf16[3,4,256,128]{3,2,1,0:T(8,128)(2,1)S(1)} %get-tuple-element.32.refs_7_.refs_4_), channel_id=1, source_target_pairs={{0,64},{64,0},{1,65},{65,1},{2,66},{66,2},{3,67},{67,3},{4,68},{68... | collective-permute-start | bytes 2359304 | tf_op jit(solution)/shard_map/ppermute | solution.py:332
  51.2 1.1 copy-done.3
  52.3 15.8 %step.3 = (f32[2,3,4,256,128]{4,3,2,1,0:T(8,128)}, bf16[2,3,4,64,128]{4,3,2,1,0:T(8,128)(2,1)}, bf16[2,3,4,64,128]{4,3,2,1,0:T(8,128)(2,1)}) custom-call(s32[1]{0:T(128)} %bitcast.10.refs_0_, f32[2,3,4,256,128]{4,3,2,1,0:T(8,128)} %copy-done.16, bf16[2,3,4,64,128]{4,3,2,1,0:T(8,128)(2,1)S(1)} %collective-permute-done.refs_2_, ...), custom_call_target="tpu_custom_call" | custom-call | flops 8999999488 | bytes 9000000 | tf_op jit(solution)/shard_map/step/pallas_call | solution.py:291
  68.2 6.0 %collective-permute-start.8 = (bf16[2,3,4,64,128]{4,3,2,1,0:T(8,128)(2,1)}, bf16[2,3,4,64,128]{4,3,2,1,0:T(8,128)(2,1)}, u32[]{:S(2)}, u32[]{:S(2)}) collective-permute-start(bf16[2,3,4,64,128]{4,3,2,1,0:T(8,128)(2,1)} %get-tuple-element.31), channel_id=1, source_target_pairs={{1,0},{2,1},{3,2},{4,3},{5,4},{6,5},{7,6},{8,7},{9,8},{10,9},{11,1... | collective-permute-start | bytes 1179656 | tf_op jit(solution)/shard_map/ppermute | solution.py:313
  74.2 6.0 %collective-permute-start.10 = (bf16[3,4,48,128]{3,2,1,0:T(8,128)(2,1)}, bf16[3,4,48,128]{3,2,1,0:T(8,128)(2,1)}, u32[]{:S(2)}, u32[]{:S(2)}) collective-permute-start(bf16[3,4,48,128]{3,2,1,0:T(8,128)(2,1)} %get-tuple-element.34), channel_id=1, source_target_pairs={{1,0},{2,1},{3,2},{4,3},{5,4},{6,5},{7,6},{8,7},{9,8},{10,9},{11,1... | collective-permute-start | bytes 442376 | tf_op jit(solution)/shard_map/ppermute | solution.py:313
  80.9 2.1 %collective-permute-done.9.refs_8_.refs_5_ = bf16[3,4,48,128]{3,2,1,0:T(8,128)(2,1)S(1)} collective-permute-done((bf16[3,4,48,128]{3,2,1,0:T(8,128)(2,1)S(1)}, bf16[3,4,48,128]{3,2,1,0:T(8,128)(2,1)S(1)}, u32[]{:S(2)}, u32[]{:S(2)}) %collective-permute-start.9) | collective-permute-done | bytes 147488 | tf_op jit(solution)/shard_map/ppermute | solution.py:312
  83.6 3.9 %collective-permute-start.13 = (bf16[3,4,48,128]{3,2,1,0:T(8,128)(2,1)}, bf16[3,4,48,128]{3,2,1,0:T(8,128)(2,1)}, u32[]{:S(2)}, u32[]{:S(2)}) collective-permute-start(bf16[3,4,48,128]{3,2,1,0:T(8,128)(2,1)} %get-tuple-element.43), channel_id=1, source_target_pairs={{1,0},{2,1},{3,2},{4,3},{5,4},{6,5},{7,6},{8,7},{9,8},{10,9},{11,1... | collective-permute-start | bytes 442376 | tf_op jit(solution)/shard_map/ppermute | solution.py:313
  90.5 0.9 copy-done.8
  91.4 15.7 %step.4 = (f32[2,3,4,256,128]{4,3,2,1,0:T(8,128)}, bf16[2,3,4,64,128]{4,3,2,1,0:T(8,128)(2,1)}, bf16[2,3,4,64,128]{4,3,2,1,0:T(8,128)(2,1)}) custom-call(s32[1]{0:T(128)} %bitcast.8.refs_0_, f32[2,3,4,256,128]{4,3,2,1,0:T(8,128)} %get-tuple-element.29.refs_1_, bf16[2,3,4,64,128]{4,3,2,1,0:T(8,128)(2,1)S(1)} %collective-permute-done.7.refs_2_, ...), custom_call_target="tpu_custom_call" | custom-call | flops 8999999488 | bytes 9000000 | tf_op jit(solution)/shard_map/step/pallas_call | solution.py:291
  107.2 6.2 %collective-permute-start.15 = (bf16[2,3,4,64,128]{4,3,2,1,0:T(8,128)(2,1)}, bf16[2,3,4,64,128]{4,3,2,1,0:T(8,128)(2,1)}, u32[]{:S(2)}, u32[]{:S(2)}) collective-permute-start(bf16[2,3,4,64,128]{4,3,2,1,0:T(8,128)(2,1)} %get-tuple-element.37), channel_id=1, source_target_pairs={{1,0},{2,1},{3,2},{4,3},{5,4},{6,5},{7,6},{8,7},{9,8},{10,9},{11,1... | collective-permute-start | bytes 1179656 | tf_op jit(solution)/shard_map/ppermute | solution.py:313
  116.5 2.4 %collective-permute-done.14.refs_2_ = bf16[2,3,4,64,128]{4,3,2,1,0:T(8,128)(2,1)S(1)} collective-permute-done((bf16[2,3,4,64,128]{4,3,2,1,0:T(8,128)(2,1)}, bf16[2,3,4,64,128]{4,3,2,1,0:T(8,128)(2,1)S(1)}, u32[]{:S(2)}, u32[]{:S(2)}) %collective-permute-start.14) | collective-permute-done | bytes 393248 | tf_op jit(solution)/shard_map/ppermute | solution.py:312
  119.0 0.7 copy-done.5
  119.7 1.0 copy-done.6
  120.7 0.9 copy-done.9
  121.6 15.6 %step.5 = (f32[2,3,4,256,128]{4,3,2,1,0:T(8,128)}, bf16[2,3,4,64,128]{4,3,2,1,0:T(8,128)(2,1)S(1)}, bf16[2,3,4,64,128]{4,3,2,1,0:T(8,128)(2,1)}) custom-call(s32[1]{0:T(128)} %bitcast.5.refs_0_, f32[2,3,4,256,128]{4,3,2,1,0:T(8,128)} %get-tuple-element.35.refs_1_, bf16[2,3,4,64,128]{4,3,2,1,0:T(8,128)(2,1)S(1)} %copy-done.6, ...), custom_call_target="tpu_custom_call" | custom-call | flops 8999999488 | bytes 9000000 | tf_op jit(solution)/shard_map/step/pallas_call | solution.py:291
  137.4 6.0 %collective-permute-start.17 = (bf16[2,3,4,64,128]{4,3,2,1,0:T(8,128)(2,1)S(1)}, bf16[2,3,4,64,128]{4,3,2,1,0:T(8,128)(2,1)S(1)}, u32[]{:S(2)}, u32[]{:S(2)}) collective-permute-start(bf16[2,3,4,64,128]{4,3,2,1,0:T(8,128)(2,1)S(1)} %get-tuple-element.40), channel_id=1, source_target_pairs={{1,0},{2,1},{3,2},{4,3},{5,4},{6,5},{7,6},{8,7},{9,8},{10,9},{11,1... | collective-permute-start | bytes 1179656 | tf_op jit(solution)/shard_map/ppermute | solution.py:313
  147.7 1.3 collective-permute-done.16.refs_2_
  149.0 0.9 copy-done.10
  149.9 1.0 copy-done.13
  150.9 17.3 %last_step.1 = f32[2,3,8,32,512]{4,3,2,1,0:T(8,128)} custom-call(s32[1]{0:T(128)} %bitcast.2.refs_0_, f32[2,3,4,256,128]{4,3,2,1,0:T(8,128)} %get-tuple-element.38.refs_1_, bf16[2,3,4,64,128]{4,3,2,1,0:T(8,128)(2,1)S(1)} %collective-permute-done.16.refs_2_, bf16[2,3,4,64,128]{4,3,2,1,0:T(8,128)(2,1)S(1)} %collective-permute-done.17.refs_3_, ...), custom_call_target="tpu_custom_call" | custom-call | flops 8999999488 | bytes 9000000 | tf_op jit(solution)/shard_map/last_step/pallas_call | solution.py:291
  (52 shorter events, 6.8 us)
Async XLA Ops:
  5.8 1.4 copy-start
  7.2 1.0 copy-start.14
  10.3 9.4 %copy-start.2 = (bf16[3,4,256,128]{3,2,1,0:T(8,128)(2,1)}, bf16[3,4,256,128]{3,2,1,0:T(8,128)(2,1)S(1)}, u32[]{:S(2)}) copy-start(bf16[3,4,256,128]{3,2,1,0:T(8,128)(2,1)S(1)} %get-tuple-element.26.refs_4_) | copy-start | bytes 2359300
  10.3 33.3 %copy-start.1 = (bf16[2,3,8,32,512]{4,3,2,1,0:T(8,128)(2,1)S(1)}, bf16[2,3,8,32,512]{4,3,2,1,0:T(8,128)(2,1)}, u32[]{:S(2)}) copy-start(bf16[2,3,8,32,512]{4,3,2,1,0:T(8,128)(2,1)} %traj_ref.3) | copy-start | bytes 4718596
  10.3 26.6 %collective-permute-start.4 = (bf16[3,4,256,128]{3,2,1,0:T(8,128)(2,1)S(1)}, bf16[3,4,256,128]{3,2,1,0:T(8,128)(2,1)S(1)}, u32[]{:S(2)}, u32[]{:S(2)}) collective-permute-start(bf16[3,4,256,128]{3,2,1,0:T(8,128)(2,1)S(1)} %get-tuple-element.26.refs_4_), channel_id=1, source_target_pairs={{0,64},{64,0},{1,65},{65,1},{2,66},{66,2},{3,67},{67,3},{4,68},{68... | collective-permute-start | bytes 2359304 | tf_op jit(solution)/shard_map/ppermute | solution.py:332
  19.7 1.7 copy-start.16
  21.4 29.8 %collective-permute-start = (bf16[2,3,4,64,128]{4,3,2,1,0:T(8,128)(2,1)}, bf16[2,3,4,64,128]{4,3,2,1,0:T(8,128)(2,1)S(1)}, u32[]{:S(2)}, u32[]{:S(2)}) collective-permute-start(bf16[2,3,4,64,128]{4,3,2,1,0:T(8,128)(2,1)} %get-tuple-element.24), channel_id=1, source_target_pairs={{0,1},{1,2},{2,3},{3,4},{4,5},{5,6},{6,7},{7,8},{8,9},{9,10},{10,1... | collective-permute-start | bytes 1179656 | tf_op jit(solution)/shard_map/ppermute | solution.py:312
  21.4 29.8 %collective-permute-start.1 = (bf16[2,3,4,64,128]{4,3,2,1,0:T(8,128)(2,1)}, bf16[2,3,4,64,128]{4,3,2,1,0:T(8,128)(2,1)}, u32[]{:S(2)}, u32[]{:S(2)}) collective-permute-start(bf16[2,3,4,64,128]{4,3,2,1,0:T(8,128)(2,1)} %get-tuple-element.25), channel_id=1, source_target_pairs={{1,0},{2,1},{3,2},{4,3},{5,4},{6,5},{7,6},{8,7},{9,8},{10,9},{11,1... | collective-permute-start | bytes 1179656 | tf_op jit(solution)/shard_map/ppermute | solution.py:313
  27.3 10.3 %collective-permute-start.2 = (bf16[3,4,48,128]{3,2,1,0:T(8,128)(2,1)}, bf16[3,4,48,128]{3,2,1,0:T(8,128)(2,1)}, u32[]{:S(2)}, u32[]{:S(2)}) collective-permute-start(bf16[3,4,48,128]{3,2,1,0:T(8,128)(2,1)} %get-tuple-element.27), channel_id=1, source_target_pairs={{0,1},{1,2},{2,3},{3,4},{4,5},{5,6},{6,7},{7,8},{8,9},{9,10},{10,1... | collective-permute-start | bytes 442376 | tf_op jit(solution)/shard_map/ppermute | solution.py:312
  27.3 20.5 %collective-permute-start.3 = (bf16[3,4,48,128]{3,2,1,0:T(8,128)(2,1)}, bf16[3,4,48,128]{3,2,1,0:T(8,128)(2,1)}, u32[]{:S(2)}, u32[]{:S(2)}) collective-permute-start(bf16[3,4,48,128]{3,2,1,0:T(8,128)(2,1)} %get-tuple-element.28), channel_id=1, source_target_pairs={{1,0},{2,1},{3,2},{4,3},{5,4},{6,5},{7,6},{8,7},{9,8},{10,9},{11,1... | collective-permute-start | bytes 442376 | tf_op jit(solution)/shard_map/ppermute | solution.py:313
  37.6 13.6 %collective-permute-start.5 = (bf16[3,4,48,128]{3,2,1,0:T(8,128)(2,1)}, bf16[3,4,48,128]{3,2,1,0:T(8,128)(2,1)}, u32[]{:S(2)}, u32[]{:S(2)}) collective-permute-start(bf16[3,4,48,128]{3,2,1,0:T(8,128)(2,1)} %get-tuple-element.46), channel_id=1, source_target_pairs={{0,1},{1,2},{2,3},{3,4},{4,5},{5,6},{6,7},{7,8},{8,9},{9,10},{10,1... | collective-permute-start | bytes 442376 | tf_op jit(solution)/shard_map/ppermute | solution.py:312
  37.6 13.6 %collective-permute-start.6 = (bf16[3,4,48,128]{3,2,1,0:T(8,128)(2,1)}, bf16[3,4,48,128]{3,2,1,0:T(8,128)(2,1)}, u32[]{:S(2)}, u32[]{:S(2)}) collective-permute-start(bf16[3,4,48,128]{3,2,1,0:T(8,128)(2,1)} %get-tuple-element.45), channel_id=1, source_target_pairs={{1,0},{2,1},{3,2},{4,3},{5,4},{6,5},{7,6},{8,7},{9,8},{10,9},{11,1... | collective-permute-start | bytes 442376 | tf_op jit(solution)/shard_map/ppermute | solution.py:313
  43.6 1.0 copy-start.15
  47.8 32.3 %collective-permute-start.11 = (bf16[3,4,256,128]{3,2,1,0:T(8,128)(2,1)S(1)}, bf16[3,4,256,128]{3,2,1,0:T(8,128)(2,1)S(1)}, u32[]{:S(2)}, u32[]{:S(2)}) collective-permute-start(bf16[3,4,256,128]{3,2,1,0:T(8,128)(2,1)S(1)} %get-tuple-element.32.refs_7_.refs_4_), channel_id=1, source_target_pairs={{0,64},{64,0},{1,65},{65,1},{2,66},{66,2},{3,67},{67,3},{4,68},{68... | collective-permute-start | bytes 2359304 | tf_op jit(solution)/shard_map/ppermute | solution.py:332
  51.2 1.1 copy-start.3
  52.3 21.9 %copy-start.12 = (bf16[3,4,48,128]{3,2,1,0:T(8,128)(2,1)S(1)}, bf16[3,4,48,128]{3,2,1,0:T(8,128)(2,1)}, u32[]{:S(2)}) copy-start(bf16[3,4,48,128]{3,2,1,0:T(8,128)(2,1)} %copy-done.11) | copy-start | bytes 442372
  52.3 38.2 %copy-start.4 = (bf16[3,4,256,128]{3,2,1,0:T(8,128)(2,1)S(1)}, bf16[3,4,256,128]{3,2,1,0:T(8,128)(2,1)}, u32[]{:S(2)}) copy-start(bf16[3,4,256,128]{3,2,1,0:T(8,128)(2,1)} %copy-done.2) | copy-start | bytes 2359300
  68.1 22.4 %collective-permute-start.7 = (bf16[2,3,4,64,128]{4,3,2,1,0:T(8,128)(2,1)}, bf16[2,3,4,64,128]{4,3,2,1,0:T(8,128)(2,1)S(1)}, u32[]{:S(2)}, u32[]{:S(2)}) collective-permute-start(bf16[2,3,4,64,128]{4,3,2,1,0:T(8,128)(2,1)} %get-tuple-element.30), channel_id=1, source_target_pairs={{0,1},{1,2},{2,3},{3,4},{4,5},{5,6},{6,7},{7,8},{8,9},{9,10},{10,1... | collective-permute-start | bytes 1179656 | tf_op jit(solution)/shard_map/ppermute | solution.py:312
  68.2 22.3 %collective-permute-start.8 = (bf16[2,3,4,64,128]{4,3,2,1,0:T(8,128)(2,1)}, bf16[2,3,4,64,128]{4,3,2,1,0:T(8,128)(2,1)}, u32[]{:S(2)}, u32[]{:S(2)}) collective-permute-start(bf16[2,3,4,64,128]{4,3,2,1,0:T(8,128)(2,1)} %get-tuple-element.31), channel_id=1, source_target_pairs={{1,0},{2,1},{3,2},{4,3},{5,4},{6,5},{7,6},{8,7},{9,8},{10,9},{11,1... | collective-permute-start | bytes 1179656 | tf_op jit(solution)/shard_map/ppermute | solution.py:313
  74.2 8.8 %collective-permute-start.9 = (bf16[3,4,48,128]{3,2,1,0:T(8,128)(2,1)S(1)}, bf16[3,4,48,128]{3,2,1,0:T(8,128)(2,1)S(1)}, u32[]{:S(2)}, u32[]{:S(2)}) collective-permute-start(bf16[3,4,48,128]{3,2,1,0:T(8,128)(2,1)S(1)} %copy-done.12), channel_id=1, source_target_pairs={{0,1},{1,2},{2,3},{3,4},{4,5},{5,6},{6,7},{7,8},{8,9},{9,10},{10,1... | collective-permute-start | bytes 442376 | tf_op jit(solution)/shard_map/ppermute | solution.py:312
  74.2 15.9 %collective-permute-start.10 = (bf16[3,4,48,128]{3,2,1,0:T(8,128)(2,1)}, bf16[3,4,48,128]{3,2,1,0:T(8,128)(2,1)}, u32[]{:S(2)}, u32[]{:S(2)}) collective-permute-start(bf16[3,4,48,128]{3,2,1,0:T(8,128)(2,1)} %get-tuple-element.34), channel_id=1, source_target_pairs={{1,0},{2,1},{3,2},{4,3},{5,4},{6,5},{7,6},{8,7},{9,8},{10,9},{11,1... | collective-permute-start | bytes 442376 | tf_op jit(solution)/shard_map/ppermute | solution.py:313
  80.9 9.2 %collective-permute-start.12 = (bf16[3,4,48,128]{3,2,1,0:T(8,128)(2,1)}, bf16[3,4,48,128]{3,2,1,0:T(8,128)(2,1)}, u32[]{:S(2)}, u32[]{:S(2)}) collective-permute-start(bf16[3,4,48,128]{3,2,1,0:T(8,128)(2,1)} %get-tuple-element.44), channel_id=1, source_target_pairs={{0,1},{1,2},{2,3},{3,4},{4,5},{5,6},{6,7},{7,8},{8,9},{9,10},{10,1... | collective-permute-start | bytes 442376 | tf_op jit(solution)/shard_map/ppermute | solution.py:312
  83.6 6.9 %collective-permute-start.13 = (bf16[3,4,48,128]{3,2,1,0:T(8,128)(2,1)}, bf16[3,4,48,128]{3,2,1,0:T(8,128)(2,1)}, u32[]{:S(2)}, u32[]{:S(2)}) collective-permute-start(bf16[3,4,48,128]{3,2,1,0:T(8,128)(2,1)} %get-tuple-element.43), channel_id=1, source_target_pairs={{1,0},{2,1},{3,2},{4,3},{5,4},{6,5},{7,6},{8,7},{9,8},{10,9},{11,1... | collective-permute-start | bytes 442376 | tf_op jit(solution)/shard_map/ppermute | solution.py:313
  90.5 0.9 copy-start.8
  107.1 11.9 %collective-permute-start.14 = (bf16[2,3,4,64,128]{4,3,2,1,0:T(8,128)(2,1)}, bf16[2,3,4,64,128]{4,3,2,1,0:T(8,128)(2,1)S(1)}, u32[]{:S(2)}, u32[]{:S(2)}) collective-permute-start(bf16[2,3,4,64,128]{4,3,2,1,0:T(8,128)(2,1)} %get-tuple-element.36), channel_id=1, source_target_pairs={{0,1},{1,2},{2,3},{3,4},{4,5},{5,6},{6,7},{7,8},{8,9},{9,10},{10,1... | collective-permute-start | bytes 1179656 | tf_op jit(solution)/shard_map/ppermute | solution.py:312
  107.2 12.5 %collective-permute-start.15 = (bf16[2,3,4,64,128]{4,3,2,1,0:T(8,128)(2,1)}, bf16[2,3,4,64,128]{4,3,2,1,0:T(8,128)(2,1)}, u32[]{:S(2)}, u32[]{:S(2)}) collective-permute-start(bf16[2,3,4,64,128]{4,3,2,1,0:T(8,128)(2,1)} %get-tuple-element.37), channel_id=1, source_target_pairs={{1,0},{2,1},{3,2},{4,3},{5,4},{6,5},{7,6},{8,7},{9,8},{10,9},{11,1... | collective-permute-start | bytes 1179656 | tf_op jit(solution)/shard_map/ppermute | solution.py:313
  119.7 1.0 copy-start.6
  120.7 0.9 copy-start.9
  137.3 11.7 %collective-permute-start.16 = (bf16[2,3,4,64,128]{4,3,2,1,0:T(8,128)(2,1)}, bf16[2,3,4,64,128]{4,3,2,1,0:T(8,128)(2,1)S(1)}, u32[]{:S(2)}, u32[]{:S(2)}) collective-permute-start(bf16[2,3,4,64,128]{4,3,2,1,0:T(8,128)(2,1)} %get-tuple-element.39), channel_id=1, source_target_pairs={{0,1},{1,2},{2,3},{3,4},{4,5},{5,6},{6,7},{7,8},{8,9},{9,10},{10,1... | collective-permute-start | bytes 1179656 | tf_op jit(solution)/shard_map/ppermute | solution.py:312
  137.4 11.6 %collective-permute-start.17 = (bf16[2,3,4,64,128]{4,3,2,1,0:T(8,128)(2,1)S(1)}, bf16[2,3,4,64,128]{4,3,2,1,0:T(8,128)(2,1)S(1)}, u32[]{:S(2)}, u32[]{:S(2)}) collective-permute-start(bf16[2,3,4,64,128]{4,3,2,1,0:T(8,128)(2,1)S(1)} %get-tuple-element.40), channel_id=1, source_target_pairs={{1,0},{2,1},{3,2},{4,3},{5,4},{6,5},{7,6},{8,7},{9,8},{10,9},{11,1... | collective-permute-start | bytes 1179656 | tf_op jit(solution)/shard_map/ppermute | solution.py:313
  149.0 0.9 copy-start.10
  149.9 1.0 copy-start.13
  (3 other events, 2.1 us)
where the time goes:
time: 169 us; the launch traced here: 168 us
  Pallas kernels  74.5 us (44%)
  starting transfers between devices  52.7 us (31%)
  local copies, waits for them, and re-layouts  16.6 us (10%)
  between operations  13.3 us (8%)
  waiting for transfers between devices  9.83 us (6%)
    pallas_call x4, Pallas kernels, advance(): pl.pallas_call(functools.partial(step_kernel, choices, last), grid=(nv,),...  64.4 us
    ppermute x8, starting transfers between devices, neighbours(): lax.ppermute(head, 'tile', [((i + 1) % count, i) for i in range(count)])  45.8 us
    unnamed x34, local copies, waits for them, and re-layouts  13.1 us
    ppermute x2, starting transfers between devices, on_device(): got.append(lax.ppermute(core, 'member', swap))  6.6 us
    pallas_call x1, Pallas kernels, convert_vectors(): pl.pallas_call(vectors_kernel, grid=(nv, 3), in_specs=[pl.BlockSpec((1, 1...  6.15 us
    ppermute x8, waiting for transfers between devices, neighbours(): lax.ppermute(tail, 'tile', [(i, (i + 1) % count) for i in range(count)])  5.85 us
    pallas_call x2, Pallas kernels, convert_base(): pl.pallas_call(base_kernel, grid_spec=spec, out_shape=[jax.ShapeDtypeStru...  3.99 us
    ppermute x2, waiting for transfers between devices, on_device(): got.append(lax.ppermute(core, 'member', swap))  3.58 us
  transfers between devices with their start and end apart: 18, of which 5 were waited for; matrix products, arithmetic and copies ran while one was open for 1% of the time, Pallas kernels for 14%

commit v1 on v0

v1 whole, which is shorter than its diff:
```python
import functools

import jax
import jax.numpy as jnp
import numpy as np
from jax import lax
from jax.experimental import pallas as pl
from jax.experimental.pallas import tpu as pltpu
from jax.sharding import PartitionSpec as P

STEPS = 4
COURANT = 0.8
NK, LANES, LEV, LON, NLAT = 4, 128, 8, 32, 512
CORE = LON * LEV
WIDE = 6
RIM = WIDE * LEV
NEAR = 2 * LEV
EXT = CORE + 2 * RIM
RUN = (8, 4, 4, 4)
VMEM_LIMIT = 34 * 1024 * 1024
F32, BF16 = jnp.float32, jnp.bfloat16


def lane_order():
    order = np.zeros((NLAT, NLAT), np.float32)
    for lat in range(NLAT):
        order[lat, (lat % NK) * LANES + lat // NK] = 1.0
    return order


def dot(a, b):
    return jnp.dot(a, b, preferred_element_type=F32)


def split_dot(x, order):
    high = x.astype(BF16)
    rest = (x - high.astype(F32)).astype(BF16)
    return dot(high, order) + dot(rest, order)


def scatter_rows(y, dst):
    for lev in range(LEV):
        for tile in range(LON // 8):
            for k in range(NK):
                dst[k, pl.ds(tile * 64 + lev, 8, stride=LEV), :] = y[
                    lev * LON + tile * 8 : lev * LON + tile * 8 + 8, k * LANES : (k + 1) * LANES
                ]


def gather_rows(src):
    rows = []
    for lev in range(LEV):
        for tile in range(LON // 8):
            rows.append(
                jnp.concatenate([src[k, pl.ds(tile * 64 + lev, 8, stride=LEV), :] for k in range(NK)], axis=1)
            )
    return jnp.concatenate(rows, axis=0)


def pack_edges(p, head_ref, tail_ref, at):
    for k in range(NK):
        head = p[k, pl.ds(0, RIM), :]
        tail = p[k, pl.ds(CORE - RIM, RIM), :]
        high, last = head.astype(BF16), tail.astype(BF16)
        head_ref[(*at, k, pl.ds(0, RIM), slice(None))] = high
        head_ref[(*at, k, pl.ds(RIM, NEAR), slice(None))] = (head[:NEAR] - high[:NEAR].astype(F32)).astype(BF16)
        tail_ref[(*at, k, pl.ds(0, RIM), slice(None))] = last
        tail_ref[(*at, k, pl.ds(RIM, NEAR), slice(None))] = (tail[RIM - NEAR :] - last[RIM - NEAR :].astype(F32)).astype(BF16)


def timetable(table_ref, slots):
    me = lax.axis_index("member")
    owner = [lax.div(table_ref[s], slots) for s in range(STEPS)]
    local = [lax.rem(table_ref[s], slots) for s in range(STEPS)]
    first = jnp.where(owner[0] == me, local[0], jnp.where(owner[1] == me, local[1], local[2]))
    which = []
    for s in range(STEPS):
        rank = jnp.int32(0)
        for e in range(s):
            rank = rank + jnp.where(owner[e] == owner[s], 1, 0)
        which.append(jnp.where(owner[s] == me, rank, 2 + rank))
    return (first, 1 - first), which


def base_kernel(table_ref, traj_ref, order_ref, core_a, core_b, head_ref, tail_ref, rows):
    turns, _ = timetable(table_ref, traj_ref.shape[0])
    for turn, core_ref in enumerate((core_a, core_b)):
        for c in range(3):
            scatter_rows(dot(traj_ref[turns[turn], c].reshape(LEV * LON, NLAT), order_ref[...]), rows.at[c])
            for k in range(NK):
                core_ref[c, k] = rows[c, k].astype(BF16)
                head_ref[turn, c, k] = rows[c, k, pl.ds(0, RIM), :].astype(BF16)
                tail_ref[turn, c, k] = rows[c, k, pl.ds(CORE - RIM, RIM), :].astype(BF16)


def convert_base(table, trajectory, order):
    return pl.pallas_call(
        base_kernel,
        in_specs=[pl.BlockSpec(memory_space=pltpu.SMEM)] + [pl.BlockSpec(memory_space=pltpu.VMEM)] * 2,
        out_specs=[pl.BlockSpec(memory_space=pltpu.VMEM)] * 4,
        out_shape=[jax.ShapeDtypeStruct((3, NK, CORE, LANES), BF16)] * 2
        + [jax.ShapeDtypeStruct((2, 3, NK, RIM, LANES), BF16)] * 2,
        scratch_shapes=[pltpu.VMEM((3, NK, CORE, LANES), F32)],
        compiler_params=pltpu.CompilerParams(vmem_limit_bytes=VMEM_LIMIT),
        cost_estimate=pl.CostEstimate(flops=1_000_000, bytes_accessed=100_000, transcendentals=0),
        name="convert_base",
    )(table, trajectory, order)


def vectors_kernel(vec_ref, order_ref, core_ref, head_ref, tail_ref):
    y = split_dot(vec_ref[0, 0].reshape(LEV * LON, NLAT), order_ref[...])
    scatter_rows(y, core_ref.at[0, 0])
    pack_edges(core_ref.at[0, 0], head_ref, tail_ref, (0, 0))


def convert_vectors(vectors, order):
    nv = vectors.shape[0]
    return pl.pallas_call(
        vectors_kernel,
        grid=(nv, 3),
        in_specs=[
            pl.BlockSpec((1, 1, LEV, LON, NLAT), lambda v, c: (v, c, 0, 0, 0)),
            pl.BlockSpec((NLAT, NLAT), lambda v, c: (0, 0)),
        ],
        out_specs=[
            pl.BlockSpec((1, 1, NK, CORE, LANES), lambda v, c: (v, c, 0, 0, 0)),
            pl.BlockSpec((1, 1, NK, RIM + NEAR, LANES), lambda v, c: (v, c, 0, 0, 0)),
            pl.BlockSpec((1, 1, NK, RIM + NEAR, LANES), lambda v, c: (v, c, 0, 0, 0)),
        ],
        out_shape=[
            jax.ShapeDtypeStruct((nv, 3, NK, CORE, LANES), F32),
            jax.ShapeDtypeStruct((nv, 3, NK, RIM + NEAR, LANES), BF16),
            jax.ShapeDtypeStruct((nv, 3, NK, RIM + NEAR, LANES), BF16),
        ],
        compiler_params=pltpu.CompilerParams(vmem_limit_bytes=VMEM_LIMIT),
        cost_estimate=pl.CostEstimate(flops=1_000_000, bytes_accessed=100_000, transcendentals=0),
        name="convert_vectors",
    )(vectors, order)


def lat_difference(v, masks):
    first, last = masks
    below = jnp.where(first, 0.0, pltpu.roll(v[3], 1, axis=1))
    above = jnp.where(last, 0.0, pltpu.roll(v[0], LANES - 1, axis=1))
    return [v[1] - below, v[2] - v[0], v[3] - v[1], above - v[2]]


def lane_masks():
    lane = lax.broadcasted_iota(jnp.int32, (8, LANES), 1)
    return lane == 0, lane == LANES - 1


def derive(base, der, row, count):
    masks = lane_masks()
    for c in range(3):
        win = [[base[c, k, pl.ds(row + 8 * i - 16, 8), :] for k in range(NK)] for i in range(count + 4)]
        for i in range(count):
            at = pl.ds(row + 8 * i, 8)
            diff = lat_difference(win[i + 2], masks)
            for k in range(NK):
                dx = (8.0 * (win[i + 3][k] - win[i + 1][k]) - (win[i + 4][k] - win[i][k])) * (-COURANT / 12.0)
                dy = diff[k] * (-COURANT / 2.0)
                der[2 + c, k, at, :] = dx + 1.0 if c == 0 else dx
                der[5 + c, k, at, :] = dy + 1.0 if c == 1 else dy
                if c == 0:
                    der[0, k, at, :] = win[i + 2][k] * (-COURANT / 12.0)
                if c == 1:
                    der[1, k, at, :] = win[i + 2][k] * (-COURANT / 2.0)


def stage(src, start, der, row, count, keep, scale, put):
    masks = lane_masks()
    mid = [[[src[c, k, pl.ds(row + 8 * i, 8), :] for k in range(NK)] for i in range(count)] for c in range(2)]
    for c in range(3):
        win = [[src[c, k, pl.ds(row + 8 * i - 16, 8), :] for k in range(NK)] for i in range(count + 4)]
        for i in range(count):
            at = pl.ds(row + 8 * i, 8)
            diff = lat_difference(win[i + 2], masks)
            for k in range(NK):
                dx = 8.0 * (win[i + 3][k] - win[i + 1][k]) - (win[i + 4][k] - win[i][k])
                s = der[0, k, at, :] * dx + der[1, k, at, :] * diff[k]
                s = s + mid[0][i][k] * der[2 + c, k, at, :] + mid[1][i][k] * der[5 + c, k, at, :]
                if c == 2:
                    s = s + win[i + 2][k]
                if keep:
                    s = s + keep * start[c, k, at, :]
                if scale != 1.0:
                    s = s * scale
                put(c, k, row + 8 * i, s)


def sweep(low, high, count, body):
    rows = count * LEV

    def at(i, carry):
        body(pl.multiple_of(low + i * rows, LEV))
        return carry

    lax.fori_loop(0, (high - low) // rows, at, 0)


def widen_base(core, left, right, base):
    for c in range(3):
        for k in range(NK):
            base[c, k, pl.ds(0, RIM), :] = left[c, k].astype(F32)
            base[c, k, pl.ds(RIM, CORE), :] = core[c, k].astype(F32)
            base[c, k, pl.ds(RIM + CORE, RIM), :] = right[c, k].astype(F32)


def widen_pert(core, left, right, wide):
    for c in range(3):
        for k in range(NK):
            wide[c, k, pl.ds(RIM, CORE), :] = core[c, k]
            far = left[c, k, pl.ds(0, RIM), :].astype(F32)
            near = left[c, k, pl.ds(RIM, NEAR), :].astype(F32)
            wide[c, k, pl.ds(0, RIM - NEAR), :] = far[: RIM - NEAR]
            wide[c, k, pl.ds(RIM - NEAR, NEAR), :] = far[RIM - NEAR :] + near
            far = right[c, k, pl.ds(0, RIM), :].astype(F32)
            near = right[c, k, pl.ds(RIM, NEAR), :].astype(F32)
            wide[c, k, pl.ds(RIM + CORE, NEAR), :] = far[:NEAR] + near
            wide[c, k, pl.ds(RIM + CORE + NEAR, RIM - NEAR), :] = far[NEAR:]


def into(ref, shift=0):
    def put(c, k, row, s):
        ref[c, k, pl.ds(row - shift, LEV), :] = s

    return put


def step_kernel(step, slots, last, *refs):
    table_ref, p_ref, left_ref, right_ref, own_a, own_b, own_left, own_right = refs[:8]
    sets = [(0, own_a, own_left.at[0], own_right.at[0]), (1, own_b, own_left.at[1], own_right.at[1])]
    taken = 8
    for choice in (2, 3) if step else (2,):
        sets.append((choice, *refs[taken : taken + 3]))
        taken += 3
    rest = refs[taken:]
    if last:
        order_ref, out_ref, base, der, one, two, three = rest
    else:
        out_ref, head_ref, tail_ref, base, der, one, two, three = rest
    _, which = timetable(table_ref, slots)
    for choice, *group in sets:

        @pl.when(which[step] == choice)
        def _(group=group):
            widen_base(*group, base)

    sweep(2 * LEV, EXT - 2 * LEV, RUN[0], lambda row: derive(base, der, row, RUN[0]))

    def vector(v, carry):
        widen_pert(p_ref.at[v], left_ref.at[v], right_ref.at[v], one)
        final = two if last else out_ref.at[v]
        sweep(2 * LEV, EXT - 2 * LEV, RUN[1], lambda row: stage(one, one, der, row, RUN[1], 0.0, 1.0, into(two)))
        sweep(4 * LEV, EXT - 4 * LEV, RUN[2], lambda row: stage(two, one, der, row, RUN[2], 3.0, 1.0, into(three)))
        sweep(
            6 * LEV,
            EXT - 6 * LEV,
            RUN[3],
            lambda row: stage(three, one, der, row, RUN[3], 2.0, 1.0 / 6.0, into(final, RIM)),
        )
        for c in range(3):
            if last:
                out_ref[v, c] = split_dot(gather_rows(two.at[c]), order_ref[...]).reshape(LEV, LON, NLAT)
            else:
                pack_edges(out_ref.at[v, c], head_ref.at[v], tail_ref.at[v], (c,))
        return carry

    lax.fori_loop(0, p_ref.shape[0], vector, 0)


def advance(step, slots, table, pert, edges, bases, order):
    last = step == STEPS - 1
    nv = pert.shape[0]
    args = [table, pert, *edges, *bases]
    if last:
        args.append(order)
        out_shape = jax.ShapeDtypeStruct((nv, 3, LEV, LON, NLAT), F32)
        out_specs = pl.BlockSpec(memory_space=pltpu.VMEM)
    else:
        out_shape = [
            jax.ShapeDtypeStruct((nv, 3, NK, CORE, LANES), F32),
            jax.ShapeDtypeStruct((nv, 3, NK, RIM + NEAR, LANES), BF16),
            jax.ShapeDtypeStruct((nv, 3, NK, RIM + NEAR, LANES), BF16),
        ]
        out_specs = [pl.BlockSpec(memory_space=pltpu.VMEM)] * 3
    return pl.pallas_call(
        functools.partial(step_kernel, step, slots, last),
        in_specs=[pl.BlockSpec(memory_space=pltpu.SMEM)] + [pl.BlockSpec(memory_space=pltpu.VMEM)] * (len(args) - 1),
        out_specs=out_specs,
        out_shape=out_shape,
        scratch_shapes=[pltpu.VMEM((3, NK, EXT, LANES), F32), pltpu.VMEM((8, NK, EXT, LANES), F32)]
        + [pltpu.VMEM((3, NK, EXT, LANES), F32)] * 3,
        compiler_params=pltpu.CompilerParams(vmem_limit_bytes=VMEM_LIMIT),
        cost_estimate=pl.CostEstimate(flops=1_000_000, bytes_accessed=100_000, transcendentals=0),
        name="last_step" if last else "step",
    )(*args)


def neighbours(head, tail):
    count = lax.axis_size("tile")
    left = lax.ppermute(tail, "tile", [(i, (i + 1) % count) for i in range(count)])
    right = lax.ppermute(head, "tile", [((i + 1) % count, i) for i in range(count)])
    return left, right


def on_device(order, order_back, vectors, trajectory, slot_table):
    slots = trajectory.shape[0]
    swap = [(0, 1), (1, 0)]
    own_a, own_b, head, tail = convert_base(slot_table, trajectory, order)
    got = [lax.ppermute(core, "member", swap) for core in (own_a, own_b)]
    own = (own_a, own_b, *neighbours(head, tail))
    got = [(core, *neighbours(core[:, :, :RIM], core[:, :, CORE - RIM :])) for core in got]

    pert, head, tail = convert_vectors(vectors, order)
    for step in range(STEPS):
        edges = neighbours(head, tail)
        bases = (*own, *got[0], *got[1]) if step else (*own, *got[0])
        done = advance(step, slots, slot_table, pert, edges, bases, order_back)
        if step == STEPS - 1:
            return done
        pert, head, tail = done


def solution(mesh):
    order = lane_order()

    def program(vectors, trajectory, slot_table):
        body = functools.partial(on_device, jnp.asarray(order, BF16), jnp.asarray(order.T, BF16))
        spec = P("member", None, None, "tile", None)
        return jax.shard_map(body, mesh=mesh, in_specs=(spec, spec, P()), out_specs=spec, check_vma=False)(
            vectors, trajectory, slot_table
        )

    return program
```

time: 169 us -> 120 us (0.71)
  Pallas kernels: 74.5 us -> 40.6 us
  waiting for transfers between devices: 9.83 us -> 41.4 us
  starting transfers between devices: 52.7 us -> 31.9 us
  between operations: 13.3 us -> 0.12 us
  local copies, waits for them, and re-layouts: 16.6 us -> 6.08 us
    pallas_call x6 -> x5, Pallas kernels: 68.4 us -> 37.4 us  [the longest x4 35.5 us: advance(): pl.pallas_call(functools.partial(step_kernel, step, slots, last), in_spec...]
    ppermute x8 -> x7, starting transfers between devices: 45.8 us -> 27.5 us  [neighbours(): lax.ppermute(head, 'tile', [((i + 1) % count, i) for i in range(count)])]
    ppermute x8 -> x7, waiting for transfers between devices: 5.85 us -> 17.7 us  [neighbours(): lax.ppermute(tail, 'tile', [(i, (i + 1) % count) for i in range(count)])]
    ppermute x8 -> x7, waiting for transfers between devices: 0.4 us -> 10.4 us  [neighbours(): lax.ppermute(head, 'tile', [((i + 1) % count, i) for i in range(count)])]
    ppermute x2, waiting for transfers between devices: 3.58 us -> 13.3 us  [on_device(): got = [lax.ppermute(core, 'member', swap) for core in (own_a, own_b)]]
    unnamed x34 -> x14, local copies, waits for them, and re-layouts: 13.1 us -> 6.04 us
    ppermute x2, starting transfers between devices: 6.6 us -> 3.61 us  [on_device(): got = [lax.ppermute(core, 'member', swap) for core in (own_a, own_b)]]
    pallas_call x1, Pallas kernels: 6.15 us -> 3.19 us  [convert_vectors(): pl.pallas_call(vectors_kernel, grid=(nv, 3), in_specs=[pl.BlockSpec((1, 1...]
  transfers between devices with their start and end apart: 18 -> 16, of which waited for: 5 -> 8; matrix products, arithmetic and copies ran while one was open for 1% -> 0% of each run, Pallas kernels for 14% -> 9%
where the time goes in v1:
time: 120 us
  waiting for transfers between devices  41.4 us (34%)
  Pallas kernels  40.6 us (34%)
  starting transfers between devices  31.9 us (27%)
  local copies, waits for them, and re-layouts  6.08 us (5%)
    pallas_call x4, Pallas kernels, advance(): pl.pallas_call(functools.partial(step_kernel, step, slots, last), in_spec...  35.5 us
    ppermute x7, starting transfers between devices, neighbours(): lax.ppermute(head, 'tile', [((i + 1) % count, i) for i in range(count)])  27.5 us
    ppermute x7, waiting for transfers between devices, neighbours(): lax.ppermute(tail, 'tile', [(i, (i + 1) % count) for i in range(count)])  17.7 us
    ppermute x2, waiting for transfers between devices, on_device(): got = [lax.ppermute(core, 'member', swap) for core in (own_a, own_b)]  13.3 us
    ppermute x7, waiting for transfers between devices, neighbours(): lax.ppermute(head, 'tile', [((i + 1) % count, i) for i in range(count)])  10.4 us
    unnamed x14, local copies, waits for them, and re-layouts  6.04 us
    ppermute x2, starting transfers between devices, on_device(): got = [lax.ppermute(core, 'member', swap) for core in (own_a, own_b)]  3.61 us
    pallas_call x1, Pallas kernels, convert_vectors(): pl.pallas_call(vectors_kernel, grid=(nv, 3), in_specs=[pl.BlockSpec((1, 1...  3.19 us
  transfers between devices with their start and end apart: 16, of which 8 were waited for; matrix products, arithmetic and copies ran while one was open for 0% of the time, Pallas kernels for 9%

profile of v1, /device:TPU:0, one launch (start us, length us, event | category | flops | bytes accessed | tf_op | source)
XLA Modules:
  0.0 120.2 jit_solution(517398907575098386)
XLA Ops:
  0.0 1.0 copy-done.1
  1.0 1.4 %copy-done.3 = bf16[2,3,8,32,512]{4,3,2,1,0:T(8,128)(2,1)S(1)} copy-done((bf16[2,3,8,32,512]{4,3,2,1,0:T(8,128)(2,1)S(1)}, bf16[2,3,8,32,512]{4,3,2,1,0:T(8,128)(2,1)}, u32[]{:S(2)}) %copy-start.3) | copy-done | bytes 1572888
  2.5 0.7 copy-done.5
  3.1 1.9 %convert_base.1 = (bf16[3,4,256,128]{3,2,1,0:T(8,128)(2,1)S(1)}, bf16[3,4,256,128]{3,2,1,0:T(8,128)(2,1)S(1)}, bf16[2,3,4,48,128]{4,3,2,1,0:T(8,128)(2,1)S(1)}, bf16[2,3,4,48,128]{4,3,2,1,0:T(8,128)(2,1)S(1)}) custom-call(s32[4]{0:T(128)S(1)} %copy-done.5, bf16[2,3,8,32,512]{4,3,2,1,0:T(8,128)(2,1)S(1)} %copy-done.3, bf16[512,512]{1,0:T(8,128)(2,1)S(1)} %copy-done.1), custom_call_target="tpu_custom_call" | custom-call | flops 1000000 | bytes 100000 | tf_op jit(solution)/shard_map/convert_base/pallas_call | solution.py:97
  5.1 3.4 %collective-permute-start.4 = (bf16[3,4,256,128]{3,2,1,0:T(8,128)(2,1)S(1)}, bf16[3,4,256,128]{3,2,1,0:T(8,128)(2,1)S(1)}, u32[]{:S(2)}, u32[]{:S(2)}) collective-permute-start(bf16[3,4,256,128]{3,2,1,0:T(8,128)(2,1)S(1)} %get-tuple-element.24.refs_4_), channel_id=1, source_target_pairs={{0,64},{64,0},{1,65},{65,1},{2,66},{66,2},{3,67},{67,3},{4,68},{68... | collective-permute-start | bytes 2359304 | tf_op jit(solution)/shard_map/ppermute | solution.py:312
  8.4 0.2 collective-permute-start.9
  8.7 6.2 %collective-permute-start.3 = (bf16[2,3,4,48,128]{4,3,2,1,0:T(8,128)(2,1)S(1)}, bf16[2,3,4,48,128]{4,3,2,1,0:T(8,128)(2,1)S(1)}, u32[]{:S(2)}, u32[]{:S(2)}) collective-permute-start(bf16[2,3,4,48,128]{4,3,2,1,0:T(8,128)(2,1)S(1)} %get-tuple-element.27), channel_id=1, source_target_pairs={{1,0},{2,1},{3,2},{4,3},{5,4},{6,5},{7,6},{8,7},{9,8},{10,9},{11,1... | collective-permute-start | bytes 884744 | tf_op jit(solution)/shard_map/ppermute | solution.py:304
  14.9 1.9 %copy-done = f32[2,3,8,32,512]{4,3,2,1,0:T(8,128)S(1)} copy-done((f32[2,3,8,32,512]{4,3,2,1,0:T(8,128)S(1)}, f32[2,3,8,32,512]{4,3,2,1,0:T(8,128)}, u32[]{:S(2)}) %copy-start) | copy-done | bytes 3145752
  16.8 1.0 copy-done.2
  17.8 3.2 %convert_vectors.1 = (f32[2,3,4,256,128]{4,3,2,1,0:T(8,128)S(1)}, bf16[2,3,4,64,128]{4,3,2,1,0:T(8,128)(2,1)S(1)}, bf16[2,3,4,64,128]{4,3,2,1,0:T(8,128)(2,1)S(1)}) custom-call(f32[2,3,8,32,512]{4,3,2,1,0:T(8,128)S(1)} %copy-done, bf16[512,512]{1,0:T(8,128)(2,1)S(1)} %copy-done.2), custom_call_target="tpu_custom_call" | custom-call | flops 1000000 | bytes 100000 | tf_op jit(solution)/shard_map/convert_vectors/pallas_call | solution.py:118
  21.0 0.1 collective-permute-start
  21.1 13.3 %collective-permute-done.4.refs_8_ = bf16[3,4,256,128]{3,2,1,0:T(8,128)(2,1)S(1)} collective-permute-done((bf16[3,4,256,128]{3,2,1,0:T(8,128)(2,1)S(1)}, bf16[3,4,256,128]{3,2,1,0:T(8,128)(2,1)S(1)}, u32[]{:S(2)}, u32[]{:S(2)}) %collective-permute-start.4) | collective-permute-done | bytes 786464 | tf_op jit(solution)/shard_map/ppermute | solution.py:312
  34.4 0.6 collective-permute-start.1
  35.0 2.8 %collective-permute-start.6 = (bf16[3,4,48,128]{3,2,1,0:T(8,128)(2,1)S(1)}, bf16[3,4,48,128]{3,2,1,0:T(8,128)(2,1)S(1)}, u32[]{:S(2)}, u32[]{:S(2)}) collective-permute-start(bf16[3,4,48,128]{3,2,1,0:T(8,128)(2,1)S(1)} %get-tuple-element.39), channel_id=1, source_target_pairs={{1,0},{2,1},{3,2},{4,3},{5,4},{6,5},{7,6},{8,7},{9,8},{10,9},{11,1... | collective-permute-start | bytes 442376 | tf_op jit(solution)/shard_map/ppermute | solution.py:304
  37.8 2.5 %collective-permute-done.1.refs_3_ = bf16[2,3,4,64,128]{4,3,2,1,0:T(8,128)(2,1)S(1)} collective-permute-done((bf16[2,3,4,64,128]{4,3,2,1,0:T(8,128)(2,1)S(1)}, bf16[2,3,4,64,128]{4,3,2,1,0:T(8,128)(2,1)S(1)}, u32[]{:S(2)}, u32[]{:S(2)}) %collective-permute-start.1) | collective-permute-done | bytes 393248 | tf_op jit(solution)/shard_map/ppermute | solution.py:304
  40.3 1.6 %collective-permute-done.6.refs_10_ = bf16[3,4,48,128]{3,2,1,0:T(8,128)(2,1)S(1)} collective-permute-done((bf16[3,4,48,128]{3,2,1,0:T(8,128)(2,1)S(1)}, bf16[3,4,48,128]{3,2,1,0:T(8,128)(2,1)S(1)}, u32[]{:S(2)}, u32[]{:S(2)}) %collective-permute-start.6) | collective-permute-done | bytes 147488 | tf_op jit(solution)/shard_map/ppermute | solution.py:304
  41.9 4.8 %collective-permute-done.5.refs_9_ = bf16[3,4,48,128]{3,2,1,0:T(8,128)(2,1)S(1)} collective-permute-done((bf16[3,4,48,128]{3,2,1,0:T(8,128)(2,1)S(1)}, bf16[3,4,48,128]{3,2,1,0:T(8,128)(2,1)S(1)}, u32[]{:S(2)}, u32[]{:S(2)}) %collective-permute-start.5) | collective-permute-done | bytes 147488 | tf_op jit(solution)/shard_map/ppermute | solution.py:303
  46.7 8.0 %step.3 = (f32[2,3,4,256,128]{4,3,2,1,0:T(8,128)S(1)}, bf16[2,3,4,64,128]{4,3,2,1,0:T(8,128)(2,1)S(1)}, bf16[2,3,4,64,128]{4,3,2,1,0:T(8,128)(2,1)S(1)}) custom-call(s32[4]{0:T(128)S(1)} %copy-done.6, f32[2,3,4,256,128]{4,3,2,1,0:T(8,128)S(1)} %get-tuple-element.21.refs_1_, bf16[2,3,4,64,128]{4,3,2,1,0:T(8,128)(2,1)S(1)} %collective-permute-done.refs_2_, ...), custom_call_target="tpu_custom_call" | custom-call | flops 1000000 | bytes 100000 | tf_op jit(solution)/shard_map/step/pallas_call | solution.py:288
  54.7 0.1 collective-permute-start.7
  54.8 6.0 %collective-permute-start.8 = (bf16[2,3,4,64,128]{4,3,2,1,0:T(8,128)(2,1)S(1)}, bf16[2,3,4,64,128]{4,3,2,1,0:T(8,128)(2,1)S(1)}, u32[]{:S(2)}, u32[]{:S(2)}) collective-permute-start(bf16[2,3,4,64,128]{4,3,2,1,0:T(8,128)(2,1)S(1)} %get-tuple-element.30), channel_id=1, source_target_pairs={{1,0},{2,1},{3,2},{4,3},{5,4},{6,5},{7,6},{8,7},{9,8},{10,9},{11,1... | collective-permute-start | bytes 1179656 | tf_op jit(solution)/shard_map/ppermute | solution.py:304
  60.8 0.5 collective-permute-start.10
  61.3 6.3 %collective-permute-done.11.refs_13_ = bf16[3,4,48,128]{3,2,1,0:T(8,128)(2,1)S(1)} collective-permute-done((bf16[3,4,48,128]{3,2,1,0:T(8,128)(2,1)S(1)}, bf16[3,4,48,128]{3,2,1,0:T(8,128)(2,1)S(1)}, u32[]{:S(2)}, u32[]{:S(2)}) %collective-permute-start.11) | collective-permute-done | bytes 147488 | tf_op jit(solution)/shard_map/ppermute | solution.py:304
  67.6 2.1 %collective-permute-done.10.refs_12_ = bf16[3,4,48,128]{3,2,1,0:T(8,128)(2,1)S(1)} collective-permute-done((bf16[3,4,48,128]{3,2,1,0:T(8,128)(2,1)S(1)}, bf16[3,4,48,128]{3,2,1,0:T(8,128)(2,1)S(1)}, u32[]{:S(2)}, u32[]{:S(2)}) %collective-permute-start.10) | collective-permute-done | bytes 147488 | tf_op jit(solution)/shard_map/ppermute | solution.py:303
  69.7 8.0 %step.4 = (f32[2,3,4,256,128]{4,3,2,1,0:T(8,128)S(1)}, bf16[2,3,4,64,128]{4,3,2,1,0:T(8,128)(2,1)S(1)}, bf16[2,3,4,64,128]{4,3,2,1,0:T(8,128)(2,1)S(1)}) custom-call(s32[4]{0:T(128)S(1)} %copy-done.6, f32[2,3,4,256,128]{4,3,2,1,0:T(8,128)S(1)} %get-tuple-element.28.refs_1_, bf16[2,3,4,64,128]{4,3,2,1,0:T(8,128)(2,1)S(1)} %collective-permute-done.7.refs_2_, ...), custom_call_target="tpu_custom_call" | custom-call | flops 1000000 | bytes 100000 | tf_op jit(solution)/shard_map/step/pallas_call | solution.py:288
  77.7 0.1 collective-permute-start.12
  77.8 6.0 %collective-permute-start.13 = (bf16[2,3,4,64,128]{4,3,2,1,0:T(8,128)(2,1)S(1)}, bf16[2,3,4,64,128]{4,3,2,1,0:T(8,128)(2,1)S(1)}, u32[]{:S(2)}, u32[]{:S(2)}) collective-permute-start(bf16[2,3,4,64,128]{4,3,2,1,0:T(8,128)(2,1)S(1)} %get-tuple-element.33), channel_id=1, source_target_pairs={{1,0},{2,1},{3,2},{4,3},{5,4},{6,5},{7,6},{8,7},{9,8},{10,9},{11,1... | collective-permute-start | bytes 1179656 | tf_op jit(solution)/shard_map/ppermute | solution.py:304
  83.7 5.5 %collective-permute-done.12.refs_2_ = bf16[2,3,4,64,128]{4,3,2,1,0:T(8,128)(2,1)S(1)} collective-permute-done((bf16[2,3,4,64,128]{4,3,2,1,0:T(8,128)(2,1)S(1)}, bf16[2,3,4,64,128]{4,3,2,1,0:T(8,128)(2,1)S(1)}, u32[]{:S(2)}, u32[]{:S(2)}) %collective-permute-start.12) | collective-permute-done | bytes 393248 | tf_op jit(solution)/shard_map/ppermute | solution.py:303
  89.2 8.0 %step.5 = (f32[2,3,4,256,128]{4,3,2,1,0:T(8,128)S(1)}, bf16[2,3,4,64,128]{4,3,2,1,0:T(8,128)(2,1)S(1)}, bf16[2,3,4,64,128]{4,3,2,1,0:T(8,128)(2,1)S(1)}) custom-call(s32[4]{0:T(128)S(1)} %copy-done.6, f32[2,3,4,256,128]{4,3,2,1,0:T(8,128)S(1)} %get-tuple-element.31.refs_1_, bf16[2,3,4,64,128]{4,3,2,1,0:T(8,128)(2,1)S(1)} %collective-permute-done.12.refs_2_, ...), custom_call_target="tpu_custom_call" | custom-call | flops 1000000 | bytes 100000 | tf_op jit(solution)/shard_map/step/pallas_call | solution.py:288
  97.2 0.1 collective-permute-start.14
  97.3 6.0 %collective-permute-start.15 = (bf16[2,3,4,64,128]{4,3,2,1,0:T(8,128)(2,1)S(1)}, bf16[2,3,4,64,128]{4,3,2,1,0:T(8,128)(2,1)S(1)}, u32[]{:S(2)}, u32[]{:S(2)}) collective-permute-start(bf16[2,3,4,64,128]{4,3,2,1,0:T(8,128)(2,1)S(1)} %get-tuple-element.36), channel_id=1, source_target_pairs={{1,0},{2,1},{3,2},{4,3},{5,4},{6,5},{7,6},{8,7},{9,8},{10,9},{11,1... | collective-permute-start | bytes 1179656 | tf_op jit(solution)/shard_map/ppermute | solution.py:304
  103.3 5.4 %collective-permute-done.14.refs_2_ = bf16[2,3,4,64,128]{4,3,2,1,0:T(8,128)(2,1)S(1)} collective-permute-done((bf16[2,3,4,64,128]{4,3,2,1,0:T(8,128)(2,1)S(1)}, bf16[2,3,4,64,128]{4,3,2,1,0:T(8,128)(2,1)S(1)}, u32[]{:S(2)}, u32[]{:S(2)}) %collective-permute-start.14) | collective-permute-done | bytes 393248 | tf_op jit(solution)/shard_map/ppermute | solution.py:303
  108.7 11.5 %last_step.1 = f32[2,3,8,32,512]{4,3,2,1,0:T(8,128)} custom-call(s32[4]{0:T(128)S(1)} %copy-done.6, f32[2,3,4,256,128]{4,3,2,1,0:T(8,128)S(1)} %get-tuple-element.34.refs_1_, bf16[2,3,4,64,128]{4,3,2,1,0:T(8,128)(2,1)S(1)} %collective-permute-done.14.refs_2_, bf16[2,3,4,64,128]{4,3,2,1,0:T(8,128)(2,1)S(1)} %collective-permute-done.15.refs_3_, ...), custom_call_target="tpu_custom_call" | custom-call | flops 1000000 | bytes 100000 | tf_op jit(solution)/shard_map/last_step/pallas_call | solution.py:288
  (22 shorter events, 0.2 us)
Async XLA Ops:
  0.0 1.0 copy-start.1
  1.0 1.4 %copy-start.3 = (bf16[2,3,8,32,512]{4,3,2,1,0:T(8,128)(2,1)S(1)}, bf16[2,3,8,32,512]{4,3,2,1,0:T(8,128)(2,1)}, u32[]{:S(2)}) copy-start(bf16[2,3,8,32,512]{4,3,2,1,0:T(8,128)(2,1)} %traj_ref.1) | copy-start | bytes 4718596
  2.5 0.7 copy-start.5
  3.1 43.6 %copy-start.6 = (s32[4]{0:T(128)S(1)}, s32[4]{0:T(128)}, u32[]{:S(2)}) copy-start(s32[4]{0:T(128)} %refs_0_.7) | copy-start | bytes 52
  5.1 29.4 %collective-permute-start.4 = (bf16[3,4,256,128]{3,2,1,0:T(8,128)(2,1)S(1)}, bf16[3,4,256,128]{3,2,1,0:T(8,128)(2,1)S(1)}, u32[]{:S(2)}, u32[]{:S(2)}) collective-permute-start(bf16[3,4,256,128]{3,2,1,0:T(8,128)(2,1)S(1)} %get-tuple-element.24.refs_4_), channel_id=1, source_target_pairs={{0,64},{64,0},{1,65},{65,1},{2,66},{66,2},{3,67},{67,3},{4,68},{68... | collective-permute-start | bytes 2359304 | tf_op jit(solution)/shard_map/ppermute | solution.py:312
  8.4 52.3 %collective-permute-start.9 = (bf16[3,4,256,128]{3,2,1,0:T(8,128)(2,1)S(1)}, bf16[3,4,256,128]{3,2,1,0:T(8,128)(2,1)S(1)}, u32[]{:S(2)}, u32[]{:S(2)}) collective-permute-start(bf16[3,4,256,128]{3,2,1,0:T(8,128)(2,1)S(1)} %get-tuple-element.25.refs_5_), channel_id=1, source_target_pairs={{0,64},{64,0},{1,65},{65,1},{2,66},{66,2},{3,67},{67,3},{4,68},{68... | collective-permute-start | bytes 2359304 | tf_op jit(solution)/shard_map/ppermute | solution.py:312
  8.7 26.4 %collective-permute-start.2 = (bf16[2,3,4,48,128]{4,3,2,1,0:T(8,128)(2,1)S(1)}, bf16[2,3,4,48,128]{4,3,2,1,0:T(8,128)(2,1)S(1)}, u32[]{:S(2)}, u32[]{:S(2)}) collective-permute-start(bf16[2,3,4,48,128]{4,3,2,1,0:T(8,128)(2,1)S(1)} %get-tuple-element.26), channel_id=1, source_target_pairs={{0,1},{1,2},{2,3},{3,4},{4,5},{5,6},{6,7},{7,8},{8,9},{9,10},{10,1... | collective-permute-start | bytes 884744 | tf_op jit(solution)/shard_map/ppermute | solution.py:303
  8.7 29.1 %collective-permute-start.3 = (bf16[2,3,4,48,128]{4,3,2,1,0:T(8,128)(2,1)S(1)}, bf16[2,3,4,48,128]{4,3,2,1,0:T(8,128)(2,1)S(1)}, u32[]{:S(2)}, u32[]{:S(2)}) collective-permute-start(bf16[2,3,4,48,128]{4,3,2,1,0:T(8,128)(2,1)S(1)} %get-tuple-element.27), channel_id=1, source_target_pairs={{1,0},{2,1},{3,2},{4,3},{5,4},{6,5},{7,6},{8,7},{9,8},{10,9},{11,1... | collective-permute-start | bytes 884744 | tf_op jit(solution)/shard_map/ppermute | solution.py:304
  14.9 1.9 %copy-start = (f32[2,3,8,32,512]{4,3,2,1,0:T(8,128)S(1)}, f32[2,3,8,32,512]{4,3,2,1,0:T(8,128)}, u32[]{:S(2)}) copy-start(f32[2,3,8,32,512]{4,3,2,1,0:T(8,128)} %vec_ref.1) | copy-start | bytes 9437188
  16.8 1.0 copy-start.2
  21.0 16.8 %collective-permute-start = (bf16[2,3,4,64,128]{4,3,2,1,0:T(8,128)(2,1)S(1)}, bf16[2,3,4,64,128]{4,3,2,1,0:T(8,128)(2,1)S(1)}, u32[]{:S(2)}, u32[]{:S(2)}) collective-permute-start(bf16[2,3,4,64,128]{4,3,2,1,0:T(8,128)(2,1)S(1)} %get-tuple-element.22), channel_id=1, source_target_pairs={{0,1},{1,2},{2,3},{3,4},{4,5},{5,6},{6,7},{7,8},{8,9},{9,10},{10,1... | collective-permute-start | bytes 1179656 | tf_op jit(solution)/shard_map/ppermute | solution.py:303
  34.4 5.9 %collective-permute-start.1 = (bf16[2,3,4,64,128]{4,3,2,1,0:T(8,128)(2,1)S(1)}, bf16[2,3,4,64,128]{4,3,2,1,0:T(8,128)(2,1)S(1)}, u32[]{:S(2)}, u32[]{:S(2)}) collective-permute-start(bf16[2,3,4,64,128]{4,3,2,1,0:T(8,128)(2,1)S(1)} %get-tuple-element.23), channel_id=1, source_target_pairs={{1,0},{2,1},{3,2},{4,3},{5,4},{6,5},{7,6},{8,7},{9,8},{10,9},{11,1... | collective-permute-start | bytes 1179656 | tf_op jit(solution)/shard_map/ppermute | solution.py:304
  35.0 6.9 %collective-permute-start.6 = (bf16[3,4,48,128]{3,2,1,0:T(8,128)(2,1)S(1)}, bf16[3,4,48,128]{3,2,1,0:T(8,128)(2,1)S(1)}, u32[]{:S(2)}, u32[]{:S(2)}) collective-permute-start(bf16[3,4,48,128]{3,2,1,0:T(8,128)(2,1)S(1)} %get-tuple-element.39), channel_id=1, source_target_pairs={{1,0},{2,1},{3,2},{4,3},{5,4},{6,5},{7,6},{8,7},{9,8},{10,9},{11,1... | collective-permute-start | bytes 442376 | tf_op jit(solution)/shard_map/ppermute | solution.py:304
  37.8 8.9 %collective-permute-start.5 = (bf16[3,4,48,128]{3,2,1,0:T(8,128)(2,1)S(1)}, bf16[3,4,48,128]{3,2,1,0:T(8,128)(2,1)S(1)}, u32[]{:S(2)}, u32[]{:S(2)}) collective-permute-start(bf16[3,4,48,128]{3,2,1,0:T(8,128)(2,1)S(1)} %get-tuple-element.40), channel_id=1, source_target_pairs={{0,1},{1,2},{2,3},{3,4},{4,5},{5,6},{6,7},{7,8},{8,9},{9,10},{10,1... | collective-permute-start | bytes 442376 | tf_op jit(solution)/shard_map/ppermute | solution.py:303
  54.7 15.0 %collective-permute-start.7 = (bf16[2,3,4,64,128]{4,3,2,1,0:T(8,128)(2,1)S(1)}, bf16[2,3,4,64,128]{4,3,2,1,0:T(8,128)(2,1)S(1)}, u32[]{:S(2)}, u32[]{:S(2)}) collective-permute-start(bf16[2,3,4,64,128]{4,3,2,1,0:T(8,128)(2,1)S(1)} %get-tuple-element.29), channel_id=1, source_target_pairs={{0,1},{1,2},{2,3},{3,4},{4,5},{5,6},{6,7},{7,8},{8,9},{9,10},{10,1... | collective-permute-start | bytes 1179656 | tf_op jit(solution)/shard_map/ppermute | solution.py:303
  54.8 14.9 %collective-permute-start.8 = (bf16[2,3,4,64,128]{4,3,2,1,0:T(8,128)(2,1)S(1)}, bf16[2,3,4,64,128]{4,3,2,1,0:T(8,128)(2,1)S(1)}, u32[]{:S(2)}, u32[]{:S(2)}) collective-permute-start(bf16[2,3,4,64,128]{4,3,2,1,0:T(8,128)(2,1)S(1)} %get-tuple-element.30), channel_id=1, source_target_pairs={{1,0},{2,1},{3,2},{4,3},{5,4},{6,5},{7,6},{8,7},{9,8},{10,9},{11,1... | collective-permute-start | bytes 1179656 | tf_op jit(solution)/shard_map/ppermute | solution.py:304
  60.7 6.8 %collective-permute-start.11 = (bf16[3,4,48,128]{3,2,1,0:T(8,128)(2,1)S(1)}, bf16[3,4,48,128]{3,2,1,0:T(8,128)(2,1)S(1)}, u32[]{:S(2)}, u32[]{:S(2)}) collective-permute-start(bf16[3,4,48,128]{3,2,1,0:T(8,128)(2,1)S(1)} %get-tuple-element.37), channel_id=1, source_target_pairs={{1,0},{2,1},{3,2},{4,3},{5,4},{6,5},{7,6},{8,7},{9,8},{10,9},{11,1... | collective-permute-start | bytes 442376 | tf_op jit(solution)/shard_map/ppermute | solution.py:304
  60.8 8.9 %collective-permute-start.10 = (bf16[3,4,48,128]{3,2,1,0:T(8,128)(2,1)S(1)}, bf16[3,4,48,128]{3,2,1,0:T(8,128)(2,1)S(1)}, u32[]{:S(2)}, u32[]{:S(2)}) collective-permute-start(bf16[3,4,48,128]{3,2,1,0:T(8,128)(2,1)S(1)} %get-tuple-element.38), channel_id=1, source_target_pairs={{0,1},{1,2},{2,3},{3,4},{4,5},{5,6},{6,7},{7,8},{8,9},{9,10},{10,1... | collective-permute-start | bytes 442376 | tf_op jit(solution)/shard_map/ppermute | solution.py:303
  77.7 11.5 %collective-permute-start.12 = (bf16[2,3,4,64,128]{4,3,2,1,0:T(8,128)(2,1)S(1)}, bf16[2,3,4,64,128]{4,3,2,1,0:T(8,128)(2,1)S(1)}, u32[]{:S(2)}, u32[]{:S(2)}) collective-permute-start(bf16[2,3,4,64,128]{4,3,2,1,0:T(8,128)(2,1)S(1)} %get-tuple-element.32), channel_id=1, source_target_pairs={{0,1},{1,2},{2,3},{3,4},{4,5},{5,6},{6,7},{7,8},{8,9},{9,10},{10,1... | collective-permute-start | bytes 1179656 | tf_op jit(solution)/shard_map/ppermute | solution.py:303
  77.8 11.4 %collective-permute-start.13 = (bf16[2,3,4,64,128]{4,3,2,1,0:T(8,128)(2,1)S(1)}, bf16[2,3,4,64,128]{4,3,2,1,0:T(8,128)(2,1)S(1)}, u32[]{:S(2)}, u32[]{:S(2)}) collective-permute-start(bf16[2,3,4,64,128]{4,3,2,1,0:T(8,128)(2,1)S(1)} %get-tuple-element.33), channel_id=1, source_target_pairs={{1,0},{2,1},{3,2},{4,3},{5,4},{6,5},{7,6},{8,7},{9,8},{10,9},{11,1... | collective-permute-start | bytes 1179656 | tf_op jit(solution)/shard_map/ppermute | solution.py:304
  89.2 19.5 %copy-start.4 = (bf16[512,512]{1,0:T(8,128)(2,1)S(1)}, bf16[512,512]{1,0:T(8,128)(2,1)}, u32[]{:S(2)}) copy-start(bf16[512,512]{1,0:T(8,128)(2,1)} %constant.5.clone.refs_14_) | copy-start | bytes 1572868
  97.2 11.5 %collective-permute-start.14 = (bf16[2,3,4,64,128]{4,3,2,1,0:T(8,128)(2,1)S(1)}, bf16[2,3,4,64,128]{4,3,2,1,0:T(8,128)(2,1)S(1)}, u32[]{:S(2)}, u32[]{:S(2)}) collective-permute-start(bf16[2,3,4,64,128]{4,3,2,1,0:T(8,128)(2,1)S(1)} %get-tuple-element.35), channel_id=1, source_target_pairs={{0,1},{1,2},{2,3},{3,4},{4,5},{5,6},{6,7},{7,8},{8,9},{9,10},{10,1... | collective-permute-start | bytes 1179656 | tf_op jit(solution)/shard_map/ppermute | solution.py:303
  97.3 11.4 %collective-permute-start.15 = (bf16[2,3,4,64,128]{4,3,2,1,0:T(8,128)(2,1)S(1)}, bf16[2,3,4,64,128]{4,3,2,1,0:T(8,128)(2,1)S(1)}, u32[]{:S(2)}, u32[]{:S(2)}) collective-permute-start(bf16[2,3,4,64,128]{4,3,2,1,0:T(8,128)(2,1)S(1)} %get-tuple-element.36), channel_id=1, source_target_pairs={{1,0},{2,1},{3,2},{4,3},{5,4},{6,5},{7,6},{8,7},{9,8},{10,9},{11,1... | collective-permute-start | bytes 1179656 | tf_op jit(solution)/shard_map/ppermute | solution.py:304

commit v2 on v1

--- a/solution.py
+++ b/solution.py
@@ -15,8 +15,10 @@
 WIDE = 6
 RIM = WIDE * LEV
 NEAR = 2 * LEV
-EXT = CORE + 2 * RIM
-RUN = (8, 4, 4, 4)
+RUN = 4
+SIDE = 16 * LEV
+HANDED = (((2, 8), (26, 4)), ((4, 10), (24, 2)))
+INTERIOR_FLOPS = 1_000_000
 VMEM_LIMIT = 34 * 1024 * 1024
 F32, BF16 = jnp.float32, jnp.bfloat16
 
@@ -199,70 +201,127 @@
     lax.fori_loop(0, (high - low) // rows, at, 0)
 
 
-def widen_base(core, left, right, base):
-    for c in range(3):
-        for k in range(NK):
-            base[c, k, pl.ds(0, RIM), :] = left[c, k].astype(F32)
-            base[c, k, pl.ds(RIM, CORE), :] = core[c, k].astype(F32)
-            base[c, k, pl.ds(RIM + CORE, RIM), :] = right[c, k].astype(F32)
-
-
-def widen_pert(core, left, right, wide):
-    for c in range(3):
-        for k in range(NK):
-            wide[c, k, pl.ds(RIM, CORE), :] = core[c, k]
-            far = left[c, k, pl.ds(0, RIM), :].astype(F32)
-            near = left[c, k, pl.ds(RIM, NEAR), :].astype(F32)
-            wide[c, k, pl.ds(0, RIM - NEAR), :] = far[: RIM - NEAR]
-            wide[c, k, pl.ds(RIM - NEAR, NEAR), :] = far[RIM - NEAR :] + near
-            far = right[c, k, pl.ds(0, RIM), :].astype(F32)
-            near = right[c, k, pl.ds(RIM, NEAR), :].astype(F32)
-            wide[c, k, pl.ds(RIM + CORE, NEAR), :] = far[:NEAR] + near
-            wide[c, k, pl.ds(RIM + CORE + NEAR, RIM - NEAR), :] = far[NEAR:]
+def choices_of(step):
+    return (0, 2) if step == 0 else (0, 1, 2, 3)
 
 
 def into(ref, shift=0):
     def put(c, k, row, s):
-        ref[c, k, pl.ds(row - shift, LEV), :] = s
+        ref[c, k, pl.ds(row + shift, LEV), :] = s
 
     return put
 
 
-def step_kernel(step, slots, last, *refs):
-    table_ref, p_ref, left_ref, right_ref, own_a, own_b, own_left, own_right = refs[:8]
+def rows_of(low, count):
+    return pl.ds(low * LEV, count * LEV)
+
+
+def interior_kernel(step, slots, table_ref, p_ref, *refs):
+    choices = choices_of(step)
+    cores = refs[: len(choices)]
+    out_ref, handed_ref, base, der, two, three = refs[len(choices) :]
+    _, which = timetable(table_ref, slots)
+    for choice, core in zip(choices, cores):
+
+        @pl.when(which[step] == choice)
+        def _(core=core):
+            for c in range(3):
+                for k in range(NK):
+                    base[c, k] = core[c, k].astype(F32)
+
+    sweep(2 * LEV, 30 * LEV, RUN, lambda row: derive(base, der, row, RUN))
+
+    def vector(v, carry):
+        one = p_ref.at[v]
+        last = into(out_ref.at[v])
+        sweep(2 * LEV, 30 * LEV, RUN, lambda row: stage(one, one, der, row, RUN, 0.0, 1.0, into(two)))
+        sweep(4 * LEV, 28 * LEV, RUN, lambda row: stage(two, one, der, row, RUN, 3.0, 1.0, into(three)))
+        sweep(6 * LEV, 26 * LEV, RUN, lambda row: stage(three, one, der, row, RUN, 2.0, 1.0 / 6.0, last))
+        for c in range(3):
+            for k in range(NK):
+                for i, (held, places) in enumerate(zip((two, three), HANDED)):
+                    for side, (low, _) in enumerate(places):
+                        handed_ref[v, c, k, rows_of(8 * i + 4 * side, 4), :] = held[c, k, rows_of(low, 4), :]
+        return carry
+
+    lax.fori_loop(0, p_ref.shape[0], vector, 0)
+
+
+def interior(step, slots, table, pert, cores):
+    nv = pert.shape[0]
+    args = [table, pert, *cores]
+    field = pltpu.VMEM((3, NK, CORE, LANES), F32)
+    return pl.pallas_call(
+        functools.partial(interior_kernel, step, slots),
+        in_specs=[pl.BlockSpec(memory_space=pltpu.SMEM)] + [pl.BlockSpec(memory_space=pltpu.VMEM)] * (len(args) - 1),
+        out_specs=[pl.BlockSpec(memory_space=pltpu.VMEM)] * 2,
+        out_shape=[
+            jax.ShapeDtypeStruct((nv, 3, NK, CORE, LANES), F32),
+            jax.ShapeDtypeStruct((nv, 3, NK, 16 * LEV, LANES), F32),
+        ],
+        scratch_shapes=[field, pltpu.VMEM((8, NK, CORE, LANES), F32), field, field],
+        compiler_params=pltpu.CompilerParams(vmem_limit_bytes=VMEM_LIMIT),
+        cost_estimate=pl.CostEstimate(flops=INTERIOR_FLOPS, bytes_accessed=100_000, transcendentals=0),
+        name="interior",
+    )(*args)
+
+
+def boundary_kernel(step, slots, last, *refs):
+    table_ref, p_ref, inner_ref, handed_ref, left_ref, right_ref, own_a, own_b, own_left, own_right = refs[:10]
     sets = [(0, own_a, own_left.at[0], own_right.at[0]), (1, own_b, own_left.at[1], own_right.at[1])]
-    taken = 8
+    taken = 10
     for choice in (2, 3) if step else (2,):
         sets.append((choice, *refs[taken : taken + 3]))
         taken += 3
     rest = refs[taken:]
     if last:
-        order_ref, out_ref, base, der, one, two, three = rest
+        order_ref, out_ref, base, der, one, two, three, whole = rest
     else:
         out_ref, head_ref, tail_ref, base, der, one, two, three = rest
     _, which = timetable(table_ref, slots)
-    for choice, *group in sets:
+    for choice, core, left, right in sets:
 
         @pl.when(which[step] == choice)
-        def _(group=group):
-            widen_base(*group, base)
-
-    sweep(2 * LEV, EXT - 2 * LEV, RUN[0], lambda row: derive(base, der, row, RUN[0]))
+        def _(core=core, left=left, right=right):
+            for c in range(3):
+                for k in range(NK):
+                    base[0, c, k, rows_of(0, 6), :] = left[c, k].astype(F32)
+                    base[0, c, k, rows_of(6, 10), :] = core[c, k, rows_of(0, 10), :].astype(F32)
+                    base[1, c, k, rows_of(0, 10), :] = core[c, k, rows_of(22, 10), :].astype(F32)
+                    base[1, c, k, rows_of(10, 6), :] = right[c, k].astype(F32)
+
+    for side, low in enumerate((2, 4)):
+        sweep(low * LEV, (low + 10) * LEV, 10, lambda row, side=side: derive(base.at[side], der.at[side], row, 10))
 
     def vector(v, carry):
-        widen_pert(p_ref.at[v], left_ref.at[v], right_ref.at[v], one)
-        final = two if last else out_ref.at[v]
-        sweep(2 * LEV, EXT - 2 * LEV, RUN[1], lambda row: stage(one, one, der, row, RUN[1], 0.0, 1.0, into(two)))
-        sweep(4 * LEV, EXT - 4 * LEV, RUN[2], lambda row: stage(two, one, der, row, RUN[2], 3.0, 1.0, into(three)))
-        sweep(
-            6 * LEV,
-            EXT - 6 * LEV,
-            RUN[3],
-            lambda row: stage(three, one, der, row, RUN[3], 2.0, 1.0 / 6.0, into(final, RIM)),
-        )
         for c in range(3):
+            for k in range(NK):
+                one[0, c, k, rows_of(6, 10), :] = p_ref[v, c, k, rows_of(0, 10), :]
+                high = left_ref[v, c, k, pl.ds(0, RIM), :].astype(F32)
+                rest = left_ref[v, c, k, pl.ds(RIM, NEAR), :].astype(F32)
+                one[0, c, k, pl.ds(0, RIM - NEAR), :] = high[: RIM - NEAR]
+                one[0, c, k, pl.ds(RIM - NEAR, NEAR), :] = high[RIM - NEAR :] + rest
+                one[1, c, k, rows_of(0, 10), :] = p_ref[v, c, k, rows_of(22, 10), :]
+                high = right_ref[v, c, k, pl.ds(0, RIM), :].astype(F32)
+                rest = right_ref[v, c, k, pl.ds(RIM, NEAR), :].astype(F32)
+                one[1, c, k, pl.ds(10 * LEV, NEAR), :] = high[:NEAR] + rest
+                one[1, c, k, pl.ds(10 * LEV + NEAR, RIM - NEAR), :] = high[NEAR:]
+                for i, (held, places) in enumerate(zip((two, three), HANDED)):
+                    for side, (_, low) in enumerate(places):
+                        held[side, c, k, rows_of(low, 4), :] = handed_ref[v, c, k, rows_of(8 * i + 4 * side, 4), :]
+        final = whole if last else out_ref.at[v]
+        for side, low in enumerate((2, 8)):
+            stage(one.at[side], one.at[side], der.at[side], low * LEV, 6, 0.0, 1.0, into(two.at[side]))
+        for side, low in enumerate((4, 6)):
+            stage(two.at[side], one.at[side], der.at[side], low * LEV, 6, 3.0, 1.0, into(three.at[side]))
+        for side, (low, shift) in enumerate(((6, -6), (4, 22))):
+            put = into(final, shift * LEV)
+            stage(three.at[side], one.at[side], der.at[side], low * LEV, 6, 2.0, 1.0 / 6.0, put)
+        for c in range(3):
+            for k in range(NK):
+                final[c, k, rows_of(6, 20), :] = inner_ref[v, c, k, rows_of(6, 20), :]
             if last:
-                out_ref[v, c] = split_dot(gather_rows(two.at[c]), order_ref[...]).reshape(LEV, LON, NLAT)
+                out_ref[v, c] = split_dot(gather_rows(whole.at[c]), order_ref[...]).reshape(LEV, LON, NLAT)
             else:
                 pack_edges(out_ref.at[v, c], head_ref.at[v], tail_ref.at[v], (c,))
         return carry
@@ -270,12 +329,15 @@
     lax.fori_loop(0, p_ref.shape[0], vector, 0)
 
 
-def advance(step, slots, table, pert, edges, bases, order):
+def boundary(step, slots, table, pert, inner, edges, bases, order):
     last = step == STEPS - 1
     nv = pert.shape[0]
-    args = [table, pert, *edges, *bases]
+    args = [table, pert, *inner, *edges, *bases]
+    side = pltpu.VMEM((2, 3, NK, SIDE, LANES), F32)
+    scratch = [side, pltpu.VMEM((2, 8, NK, SIDE, LANES), F32), side, side, side]
     if last:
         args.append(order)
+        scratch.append(pltpu.VMEM((3, NK, CORE, LANES), F32))
         out_shape = jax.ShapeDtypeStruct((nv, 3, LEV, LON, NLAT), F32)
         out_specs = pl.BlockSpec(memory_space=pltpu.VMEM)
     else:
@@ -286,15 +348,14 @@
         ]
         out_specs = [pl.BlockSpec(memory_space=pltpu.VMEM)] * 3
     return pl.pallas_call(
-        functools.partial(step_kernel, step, slots, last),
+        functools.partial(boundary_kernel, step, slots, last),
         in_specs=[pl.BlockSpec(memory_space=pltpu.SMEM)] + [pl.BlockSpec(memory_space=pltpu.VMEM)] * (len(args) - 1),
         out_specs=out_specs,
         out_shape=out_shape,
-        scratch_shapes=[pltpu.VMEM((3, NK, EXT, LANES), F32), pltpu.VMEM((8, NK, EXT, LANES), F32)]
-        + [pltpu.VMEM((3, NK, EXT, LANES), F32)] * 3,
+        scratch_shapes=scratch,
         compiler_params=pltpu.CompilerParams(vmem_limit_bytes=VMEM_LIMIT),
         cost_estimate=pl.CostEstimate(flops=1_000_000, bytes_accessed=100_000, transcendentals=0),
-        name="last_step" if last else "step",
+        name="last_boundary" if last else "boundary",
     )(*args)
 
 
@@ -311,16 +372,24 @@
     own_a, own_b, head, tail = convert_base(slot_table, trajectory, order)
     got = [lax.ppermute(core, "member", swap) for core in (own_a, own_b)]
     own = (own_a, own_b, *neighbours(head, tail))
-    got = [(core, *neighbours(core[:, :, :RIM], core[:, :, CORE - RIM :])) for core in got]
-
+
+    def with_halo(core):
+        return core, *neighbours(core[:, :, :RIM], core[:, :, CORE - RIM :])
+
+    got[0] = with_halo(got[0])
     pert, head, tail = convert_vectors(vectors, order)
     for step in range(STEPS):
         edges = neighbours(head, tail)
+        cores = (own_a, own_b, got[0][0], got[1][0] if step else None)
+        inner = interior(step, slots, slot_table, pert, [cores[i] for i in choices_of(step)])
         bases = (*own, *got[0], *got[1]) if step else (*own, *got[0])
-        done = advance(step, slots, slot_table, pert, edges, bases, order_back)
+        done = boundary(step, slots, slot_table, pert, inner, edges, bases, order_back)
         if step == STEPS - 1:
             return done
         pert, head, tail = done
+        if step == 0:
+            pert, second = lax.optimization_barrier((pert, got[1]))
+            got[1] = with_halo(second)
 
 
 def solution(mesh):

time: 120 us -> 104 us (0.87)
  waiting for transfers between devices: 41.4 us -> 19.1 us
  Pallas kernels: 40.6 us -> 45.4 us
  starting transfers between devices: 31.9 us -> 33.1 us
    ppermute x7, waiting for transfers between devices: 17.7 us -> 5.69 us  [neighbours(): lax.ppermute(tail, 'tile', [(i, (i + 1) % count) for i in range(count)])]
    ppermute x7, waiting for transfers between devices: 10.4 us -> 0.02 us  [neighbours(): lax.ppermute(head, 'tile', [((i + 1) % count, i) for i in range(count)])]
    pallas_call x4 -> x8, Pallas kernels: 35.5 us -> 40.3 us  [the longest x4 24.1 us: interior(): pl.pallas_call(functools.partial(interior_kernel, step, slots), in_specs=...]
    ppermute x7, starting transfers between devices: 27.5 us -> 29.2 us  [neighbours(): lax.ppermute(head, 'tile', [((i + 1) % count, i) for i in range(count)])]
  transfers between devices with their start and end apart: 16 -> 16, of which waited for: 8 -> 3; matrix products, arithmetic and copies ran while one was open for 0% -> 0% of each run, Pallas kernels for 9% -> 29%
where the time goes in v2:
time: 104 us
  Pallas kernels  45.4 us (44%)
  starting transfers between devices  33.1 us (32%)
  waiting for transfers between devices  19.1 us (18%)
  local copies, waits for them, and re-layouts  6.08 us (6%)
    ppermute x7, starting transfers between devices, neighbours(): lax.ppermute(head, 'tile', [((i + 1) % count, i) for i in range(count)])  29.2 us
    pallas_call x4, Pallas kernels, interior(): pl.pallas_call(functools.partial(interior_kernel, step, slots), in_specs=...  24.1 us
    pallas_call x4, Pallas kernels, boundary(): pl.pallas_call(functools.partial(boundary_kernel, step, slots, last), in_...  16.2 us
    ppermute x2, waiting for transfers between devices, on_device(): got = [lax.ppermute(core, 'member', swap) for core in (own_a, own_b)]  13.3 us
    unnamed x14, local copies, waits for them, and re-layouts  6.04 us
    ppermute x7, waiting for transfers between devices, neighbours(): lax.ppermute(tail, 'tile', [(i, (i + 1) % count) for i in range(count)])  5.69 us
    ppermute x2, starting transfers between devices, on_device(): got = [lax.ppermute(core, 'member', swap) for core in (own_a, own_b)]  3.61 us
    pallas_call x1, Pallas kernels, convert_vectors(): pl.pallas_call(vectors_kernel, grid=(nv, 3), in_specs=[pl.BlockSpec((1, 1...  3.19 us
  transfers between devices with their start and end apart: 16, of which 3 were waited for; matrix products, arithmetic and copies ran while one was open for 0% of the time, Pallas kernels for 29%

profile of v2, /device:TPU:0, one launch (start us, length us, event | category | flops | bytes accessed | tf_op | source)
XLA Modules:
  0.0 103.9 jit_solution(7295520844139299535)
XLA Ops:
  0.0 1.0 %copy-done.1 = bf16[512,512]{1,0:T(8,128)(2,1)S(1)} copy-done((bf16[512,512]{1,0:T(8,128)(2,1)S(1)}, bf16[512,512]{1,0:T(8,128)(2,1)}, u32[]{:S(2)}) %copy-start.1) | copy-done | bytes 524312
  1.0 1.4 %copy-done.3 = bf16[2,3,8,32,512]{4,3,2,1,0:T(8,128)(2,1)S(1)} copy-done((bf16[2,3,8,32,512]{4,3,2,1,0:T(8,128)(2,1)S(1)}, bf16[2,3,8,32,512]{4,3,2,1,0:T(8,128)(2,1)}, u32[]{:S(2)}) %copy-start.3) | copy-done | bytes 1572888
  2.5 0.7 copy-done.5
  3.1 1.9 %convert_base.1 = (bf16[3,4,256,128]{3,2,1,0:T(8,128)(2,1)S(1)}, bf16[3,4,256,128]{3,2,1,0:T(8,128)(2,1)S(1)}, bf16[2,3,4,48,128]{4,3,2,1,0:T(8,128)(2,1)S(1)}, bf16[2,3,4,48,128]{4,3,2,1,0:T(8,128)(2,1)S(1)}) custom-call(s32[4]{0:T(128)S(1)} %copy-done.5, bf16[2,3,8,32,512]{4,3,2,1,0:T(8,128)(2,1)S(1)} %copy-done.3, bf16[512,512]{1,0:T(8,128)(2,1)S(1)} %copy-done.1), custom_call_target="tpu_custom_call" | custom-call | flops 1000000 | bytes 100000 | tf_op jit(solution)/shard_map/convert_base/pallas_call | solution.py:99
  5.1 3.4 %collective-permute-start = (bf16[3,4,256,128]{3,2,1,0:T(8,128)(2,1)S(1)}, bf16[3,4,256,128]{3,2,1,0:T(8,128)(2,1)S(1)}, u32[]{:S(2)}, u32[]{:S(2)}) collective-permute-start(bf16[3,4,256,128]{3,2,1,0:T(8,128)(2,1)S(1)} %get-tuple-element.32.refs_0_.refs_6_), channel_id=1, source_target_pairs={{0,64},{64,0},{1,65},{65,1},{2,66},{66,2},{3,67},{67,3},{4,68},{68... | collective-permute-start | bytes 2359304 | tf_op jit(solution)/shard_map/ppermute | solution.py:373
  8.4 0.2 collective-permute-start.7
  8.7 0.0 collective-permute-start.3
  8.7 6.2 %collective-permute-start.4 = (bf16[2,3,4,48,128]{4,3,2,1,0:T(8,128)(2,1)S(1)}, bf16[2,3,4,48,128]{4,3,2,1,0:T(8,128)(2,1)S(1)}, u32[]{:S(2)}, u32[]{:S(2)}) collective-permute-start(bf16[2,3,4,48,128]{4,3,2,1,0:T(8,128)(2,1)S(1)} %get-tuple-element.39), channel_id=1, source_target_pairs={{1,0},{2,1},{3,2},{4,3},{5,4},{6,5},{7,6},{8,7},{9,8},{10,9},{11,1... | collective-permute-start | bytes 884744 | tf_op jit(solution)/shard_map/ppermute | solution.py:365
  14.9 1.9 %copy-done = f32[2,3,8,32,512]{4,3,2,1,0:T(8,128)S(1)} copy-done((f32[2,3,8,32,512]{4,3,2,1,0:T(8,128)S(1)}, f32[2,3,8,32,512]{4,3,2,1,0:T(8,128)}, u32[]{:S(2)}) %copy-start) | copy-done | bytes 3145752
  16.8 1.0 %copy-done.2 = bf16[512,512]{1,0:T(8,128)(2,1)S(1)} copy-done((bf16[512,512]{1,0:T(8,128)(2,1)S(1)}, bf16[512,512]{1,0:T(8,128)(2,1)}, u32[]{:S(2)}) %copy-start.2) | copy-done | bytes 524312
  17.8 3.2 %convert_vectors.1 = (f32[2,3,4,256,128]{4,3,2,1,0:T(8,128)S(1)}, bf16[2,3,4,64,128]{4,3,2,1,0:T(8,128)(2,1)S(1)}, bf16[2,3,4,64,128]{4,3,2,1,0:T(8,128)(2,1)S(1)}) custom-call(f32[2,3,8,32,512]{4,3,2,1,0:T(8,128)S(1)} %copy-done, bf16[512,512]{1,0:T(8,128)(2,1)S(1)} %copy-done.2), custom_call_target="tpu_custom_call" | custom-call | flops 1000000 | bytes 100000 | tf_op jit(solution)/shard_map/convert_vectors/pallas_call | solution.py:120
  21.0 0.1 collective-permute-start.1
  21.1 13.3 %collective-permute-done.refs_1_.refs_10_.refs_2_ = bf16[3,4,256,128]{3,2,1,0:T(8,128)(2,1)S(1)} collective-permute-done((bf16[3,4,256,128]{3,2,1,0:T(8,128)(2,1)S(1)}, bf16[3,4,256,128]{3,2,1,0:T(8,128)(2,1)S(1)}, u32[]{:S(2)}, u32[]{:S(2)}) %collective-permute-start) | collective-permute-done | bytes 786464 | tf_op jit(solution)/shard_map/ppermute | solution.py:373
  34.4 0.5 collective-permute-start.2
  35.0 2.8 %collective-permute-start.6 = (bf16[3,4,48,128]{3,2,1,0:T(8,128)(2,1)S(1)}, bf16[3,4,48,128]{3,2,1,0:T(8,128)(2,1)S(1)}, u32[]{:S(2)}, u32[]{:S(2)}) collective-permute-start(bf16[3,4,48,128]{3,2,1,0:T(8,128)(2,1)S(1)} %get-tuple-element.59), channel_id=1, source_target_pairs={{1,0},{2,1},{3,2},{4,3},{5,4},{6,5},{7,6},{8,7},{9,8},{10,9},{11,1... | collective-permute-start | bytes 442376 | tf_op jit(solution)/shard_map/ppermute | solution.py:365
  37.8 6.0 %interior.4 = (f32[2,3,4,256,128]{4,3,2,1,0:T(8,128)S(1)}, f32[2,3,4,128,128]{4,3,2,1,0:T(8,128)S(1)}) custom-call(s32[4]{0:T(128)S(1)} %copy-done.6, f32[2,3,4,256,128]{4,3,2,1,0:T(8,128)S(1)} %get-tuple-element.31.p_ref.refs_1_, bf16[3,4,256,128]{3,2,1,0:T(8,128)(2,1)S(1)} %get-tuple-element.32.refs_0_.refs_6_, ...), custom_call_target="tpu_custom_call" | custom-call | flops 1000000 | bytes 100000 | tf_op jit(solution)/shard_map/interior/pallas_call | solution.py:254
  43.8 2.9 %collective-permute-done.5.refs_11_ = bf16[3,4,48,128]{3,2,1,0:T(8,128)(2,1)S(1)} collective-permute-done((bf16[3,4,48,128]{3,2,1,0:T(8,128)(2,1)S(1)}, bf16[3,4,48,128]{3,2,1,0:T(8,128)(2,1)S(1)}, u32[]{:S(2)}, u32[]{:S(2)}) %collective-permute-start.5) | collective-permute-done | bytes 147488 | tf_op jit(solution)/shard_map/ppermute | solution.py:364
  46.7 3.1 %boundary.3 = (f32[2,3,4,256,128]{4,3,2,1,0:T(8,128)S(1)}, bf16[2,3,4,64,128]{4,3,2,1,0:T(8,128)(2,1)S(1)}, bf16[2,3,4,64,128]{4,3,2,1,0:T(8,128)(2,1)S(1)}) custom-call(s32[4]{0:T(128)S(1)} %copy-done.6, f32[2,3,4,256,128]{4,3,2,1,0:T(8,128)S(1)} %get-tuple-element.31.p_ref.refs_1_, f32[2,3,4,256,128]{4,3,2,1,0:T(8,128)S(1)} %get-tuple-element.33.refs_2_, ...), custom_call_target="tpu_custom_call" | custom-call | flops 1000000 | bytes 100000 | tf_op jit(solution)/shard_map/boundary/pallas_call | solution.py:350
  49.8 0.1 collective-permute-start.8
  49.9 6.0 %collective-permute-start.9 = (bf16[2,3,4,64,128]{4,3,2,1,0:T(8,128)(2,1)S(1)}, bf16[2,3,4,64,128]{4,3,2,1,0:T(8,128)(2,1)S(1)}, u32[]{:S(2)}, u32[]{:S(2)}) collective-permute-start(bf16[2,3,4,64,128]{4,3,2,1,0:T(8,128)(2,1)S(1)} %get-tuple-element.46), channel_id=1, source_target_pairs={{1,0},{2,1},{3,2},{4,3},{5,4},{6,5},{7,6},{8,7},{9,8},{10,9},{11,1... | collective-permute-start | bytes 1179656 | tf_op jit(solution)/shard_map/ppermute | solution.py:365
  55.9 1.8 %collective-permute-start.11 = (bf16[3,4,48,128]{3,2,1,0:T(8,128)(2,1)S(1)}, bf16[3,4,48,128]{3,2,1,0:T(8,128)(2,1)S(1)}, u32[]{:S(2)}, u32[]{:S(2)}) collective-permute-start(bf16[3,4,48,128]{3,2,1,0:T(8,128)(2,1)S(1)} %get-tuple-element.57), channel_id=1, source_target_pairs={{1,0},{2,1},{3,2},{4,3},{5,4},{6,5},{7,6},{8,7},{9,8},{10,9},{11,1... | collective-permute-start | bytes 442376 | tf_op jit(solution)/shard_map/ppermute | solution.py:365
  57.7 6.0 %interior.5 = (f32[2,3,4,256,128]{4,3,2,1,0:T(8,128)S(1)}, f32[2,3,4,128,128]{4,3,2,1,0:T(8,128)S(1)}) custom-call(s32[4]{0:T(128)S(1)} %copy-done.6, f32[2,3,4,256,128]{4,3,2,1,0:T(8,128)S(1)} %get-tuple-element.41.p_ref.refs_1_, bf16[3,4,256,128]{3,2,1,0:T(8,128)(2,1)S(1)} %get-tuple-element.32.refs_0_.refs_6_, ...), custom_call_target="tpu_custom_call" | custom-call | flops 1000000 | bytes 100000 | tf_op jit(solution)/shard_map/interior/pallas_call | solution.py:254
  63.7 2.8 %collective-permute-done.10.refs_14_ = bf16[3,4,48,128]{3,2,1,0:T(8,128)(2,1)S(1)} collective-permute-done((bf16[3,4,48,128]{3,2,1,0:T(8,128)(2,1)S(1)}, bf16[3,4,48,128]{3,2,1,0:T(8,128)(2,1)S(1)}, u32[]{:S(2)}, u32[]{:S(2)}) %collective-permute-start.10) | collective-permute-done | bytes 147488 | tf_op jit(solution)/shard_map/ppermute | solution.py:364
  66.5 3.2 %boundary.4 = (f32[2,3,4,256,128]{4,3,2,1,0:T(8,128)S(1)}, bf16[2,3,4,64,128]{4,3,2,1,0:T(8,128)(2,1)S(1)}, bf16[2,3,4,64,128]{4,3,2,1,0:T(8,128)(2,1)S(1)}) custom-call(s32[4]{0:T(128)S(1)} %copy-done.6, f32[2,3,4,256,128]{4,3,2,1,0:T(8,128)S(1)} %get-tuple-element.41.p_ref.refs_1_, f32[2,3,4,256,128]{4,3,2,1,0:T(8,128)S(1)} %get-tuple-element.43.refs_2_, ...), custom_call_target="tpu_custom_call" | custom-call | flops 1000000 | bytes 100000 | tf_op jit(solution)/shard_map/boundary/pallas_call | solution.py:350
  69.7 0.1 collective-permute-start.12
  69.8 6.0 %collective-permute-start.13 = (bf16[2,3,4,64,128]{4,3,2,1,0:T(8,128)(2,1)S(1)}, bf16[2,3,4,64,128]{4,3,2,1,0:T(8,128)(2,1)S(1)}, u32[]{:S(2)}, u32[]{:S(2)}) collective-permute-start(bf16[2,3,4,64,128]{4,3,2,1,0:T(8,128)(2,1)S(1)} %get-tuple-element.51), channel_id=1, source_target_pairs={{1,0},{2,1},{3,2},{4,3},{5,4},{6,5},{7,6},{8,7},{9,8},{10,9},{11,1... | collective-permute-start | bytes 1179656 | tf_op jit(solution)/shard_map/ppermute | solution.py:365
  75.7 6.2 %interior.6 = (f32[2,3,4,256,128]{4,3,2,1,0:T(8,128)S(1)}, f32[2,3,4,128,128]{4,3,2,1,0:T(8,128)S(1)}) custom-call(s32[4]{0:T(128)S(1)} %copy-done.6, f32[2,3,4,256,128]{4,3,2,1,0:T(8,128)S(1)} %get-tuple-element.47.p_ref.refs_1_, bf16[3,4,256,128]{3,2,1,0:T(8,128)(2,1)S(1)} %get-tuple-element.32.refs_0_.refs_6_, ...), custom_call_target="tpu_custom_call" | custom-call | flops 1000000 | bytes 100000 | tf_op jit(solution)/shard_map/interior/pallas_call | solution.py:254
  81.9 3.2 %boundary.5 = (f32[2,3,4,256,128]{4,3,2,1,0:T(8,128)S(1)}, bf16[2,3,4,64,128]{4,3,2,1,0:T(8,128)(2,1)S(1)}, bf16[2,3,4,64,128]{4,3,2,1,0:T(8,128)(2,1)S(1)}) custom-call(s32[4]{0:T(128)S(1)} %copy-done.6, f32[2,3,4,256,128]{4,3,2,1,0:T(8,128)S(1)} %get-tuple-element.47.p_ref.refs_1_, f32[2,3,4,256,128]{4,3,2,1,0:T(8,128)S(1)} %get-tuple-element.48.refs_2_, ...), custom_call_target="tpu_custom_call" | custom-call | flops 1000000 | bytes 100000 | tf_op jit(solution)/shard_map/boundary/pallas_call | solution.py:350
  85.1 0.1 collective-permute-start.14
  85.2 6.0 %collective-permute-start.15 = (bf16[2,3,4,64,128]{4,3,2,1,0:T(8,128)(2,1)S(1)}, bf16[2,3,4,64,128]{4,3,2,1,0:T(8,128)(2,1)S(1)}, u32[]{:S(2)}, u32[]{:S(2)}) collective-permute-start(bf16[2,3,4,64,128]{4,3,2,1,0:T(8,128)(2,1)S(1)} %get-tuple-element.56), channel_id=1, source_target_pairs={{1,0},{2,1},{3,2},{4,3},{5,4},{6,5},{7,6},{8,7},{9,8},{10,9},{11,1... | collective-permute-start | bytes 1179656 | tf_op jit(solution)/shard_map/ppermute | solution.py:365
  91.1 6.0 %interior.7 = (f32[2,3,4,256,128]{4,3,2,1,0:T(8,128)S(1)}, f32[2,3,4,128,128]{4,3,2,1,0:T(8,128)S(1)}) custom-call(s32[4]{0:T(128)S(1)} %copy-done.6, f32[2,3,4,256,128]{4,3,2,1,0:T(8,128)S(1)} %get-tuple-element.52.p_ref.refs_1_, bf16[3,4,256,128]{3,2,1,0:T(8,128)(2,1)S(1)} %get-tuple-element.32.refs_0_.refs_6_, ...), custom_call_target="tpu_custom_call" | custom-call | flops 1000000 | bytes 100000 | tf_op jit(solution)/shard_map/interior/pallas_call | solution.py:254
  97.1 6.7 %last_boundary.1 = f32[2,3,8,32,512]{4,3,2,1,0:T(8,128)} custom-call(s32[4]{0:T(128)S(1)} %copy-done.6, f32[2,3,4,256,128]{4,3,2,1,0:T(8,128)S(1)} %get-tuple-element.52.p_ref.refs_1_, f32[2,3,4,256,128]{4,3,2,1,0:T(8,128)S(1)} %get-tuple-element.53.refs_2_, f32[2,3,4,128,128]{4,3,2,1,0:T(8,128)S(1)} %get-tuple-element.54.refs_3_, ...), custom_call_target="tpu_custom_call" | custom-call | flops 1000000 | bytes 100000 | tf_op jit(solution)/shard_map/last_boundary/pallas_call | solution.py:350
  (26 shorter events, 0.1 us)
Async XLA Ops:
  0.0 1.0 %copy-start.1 = (bf16[512,512]{1,0:T(8,128)(2,1)S(1)}, bf16[512,512]{1,0:T(8,128)(2,1)}, u32[]{:S(2)}) copy-start(bf16[512,512]{1,0:T(8,128)(2,1)} %constant.4.clone.order_ref) | copy-start | bytes 1572868
  1.0 1.4 %copy-start.3 = (bf16[2,3,8,32,512]{4,3,2,1,0:T(8,128)(2,1)S(1)}, bf16[2,3,8,32,512]{4,3,2,1,0:T(8,128)(2,1)}, u32[]{:S(2)}) copy-start(bf16[2,3,8,32,512]{4,3,2,1,0:T(8,128)(2,1)} %traj_ref.1) | copy-start | bytes 4718596
  2.5 0.7 copy-start.5
  3.1 34.7 %copy-start.6 = (s32[4]{0:T(128)S(1)}, s32[4]{0:T(128)}, u32[]{:S(2)}) copy-start(s32[4]{0:T(128)} %refs_0_.7) | copy-start | bytes 52
  5.1 29.4 %collective-permute-start = (bf16[3,4,256,128]{3,2,1,0:T(8,128)(2,1)S(1)}, bf16[3,4,256,128]{3,2,1,0:T(8,128)(2,1)S(1)}, u32[]{:S(2)}, u32[]{:S(2)}) collective-permute-start(bf16[3,4,256,128]{3,2,1,0:T(8,128)(2,1)S(1)} %get-tuple-element.32.refs_0_.refs_6_), channel_id=1, source_target_pairs={{0,64},{64,0},{1,65},{65,1},{2,66},{66,2},{3,67},{67,3},{4,68},{68... | collective-permute-start | bytes 2359304 | tf_op jit(solution)/shard_map/ppermute | solution.py:373
  8.4 47.4 %collective-permute-start.7 = (bf16[3,4,256,128]{3,2,1,0:T(8,128)(2,1)S(1)}, bf16[3,4,256,128]{3,2,1,0:T(8,128)(2,1)S(1)}, u32[]{:S(2)}, u32[]{:S(2)}) collective-permute-start(bf16[3,4,256,128]{3,2,1,0:T(8,128)(2,1)S(1)} %get-tuple-element.37.refs_7_.refs_1_), channel_id=1, source_target_pairs={{0,64},{64,0},{1,65},{65,1},{2,66},{66,2},{3,67},{67,3},{4,68},{68... | collective-permute-start | bytes 2359304 | tf_op jit(solution)/shard_map/ppermute | solution.py:373
  8.7 26.3 %collective-permute-start.3 = (bf16[2,3,4,48,128]{4,3,2,1,0:T(8,128)(2,1)S(1)}, bf16[2,3,4,48,128]{4,3,2,1,0:T(8,128)(2,1)S(1)}, u32[]{:S(2)}, u32[]{:S(2)}) collective-permute-start(bf16[2,3,4,48,128]{4,3,2,1,0:T(8,128)(2,1)S(1)} %get-tuple-element.38), channel_id=1, source_target_pairs={{0,1},{1,2},{2,3},{3,4},{4,5},{5,6},{6,7},{7,8},{8,9},{9,10},{10,1... | collective-permute-start | bytes 884744 | tf_op jit(solution)/shard_map/ppermute | solution.py:364
  8.7 29.1 %collective-permute-start.4 = (bf16[2,3,4,48,128]{4,3,2,1,0:T(8,128)(2,1)S(1)}, bf16[2,3,4,48,128]{4,3,2,1,0:T(8,128)(2,1)S(1)}, u32[]{:S(2)}, u32[]{:S(2)}) collective-permute-start(bf16[2,3,4,48,128]{4,3,2,1,0:T(8,128)(2,1)S(1)} %get-tuple-element.39), channel_id=1, source_target_pairs={{1,0},{2,1},{3,2},{4,3},{5,4},{6,5},{7,6},{8,7},{9,8},{10,9},{11,1... | collective-permute-start | bytes 884744 | tf_op jit(solution)/shard_map/ppermute | solution.py:365
  14.9 1.9 %copy-start = (f32[2,3,8,32,512]{4,3,2,1,0:T(8,128)S(1)}, f32[2,3,8,32,512]{4,3,2,1,0:T(8,128)}, u32[]{:S(2)}) copy-start(f32[2,3,8,32,512]{4,3,2,1,0:T(8,128)} %vec_ref.1) | copy-start | bytes 9437188
  16.8 1.0 %copy-start.2 = (bf16[512,512]{1,0:T(8,128)(2,1)S(1)}, bf16[512,512]{1,0:T(8,128)(2,1)}, u32[]{:S(2)}) copy-start(bf16[512,512]{1,0:T(8,128)(2,1)} %constant.4.clone.order_ref) | copy-start | bytes 1572868
  21.0 22.8 %collective-permute-start.1 = (bf16[2,3,4,64,128]{4,3,2,1,0:T(8,128)(2,1)S(1)}, bf16[2,3,4,64,128]{4,3,2,1,0:T(8,128)(2,1)S(1)}, u32[]{:S(2)}, u32[]{:S(2)}) collective-permute-start(bf16[2,3,4,64,128]{4,3,2,1,0:T(8,128)(2,1)S(1)} %get-tuple-element.35), channel_id=1, source_target_pairs={{0,1},{1,2},{2,3},{3,4},{4,5},{5,6},{6,7},{7,8},{8,9},{9,10},{10,1... | collective-permute-start | bytes 1179656 | tf_op jit(solution)/shard_map/ppermute | solution.py:364
  34.4 9.3 %collective-permute-start.2 = (bf16[2,3,4,64,128]{4,3,2,1,0:T(8,128)(2,1)S(1)}, bf16[2,3,4,64,128]{4,3,2,1,0:T(8,128)(2,1)S(1)}, u32[]{:S(2)}, u32[]{:S(2)}) collective-permute-start(bf16[2,3,4,64,128]{4,3,2,1,0:T(8,128)(2,1)S(1)} %get-tuple-element.36), channel_id=1, source_target_pairs={{1,0},{2,1},{3,2},{4,3},{5,4},{6,5},{7,6},{8,7},{9,8},{10,9},{11,1... | collective-permute-start | bytes 1179656 | tf_op jit(solution)/shard_map/ppermute | solution.py:365
  35.0 8.8 %collective-permute-start.6 = (bf16[3,4,48,128]{3,2,1,0:T(8,128)(2,1)S(1)}, bf16[3,4,48,128]{3,2,1,0:T(8,128)(2,1)S(1)}, u32[]{:S(2)}, u32[]{:S(2)}) collective-permute-start(bf16[3,4,48,128]{3,2,1,0:T(8,128)(2,1)S(1)} %get-tuple-element.59), channel_id=1, source_target_pairs={{1,0},{2,1},{3,2},{4,3},{5,4},{6,5},{7,6},{8,7},{9,8},{10,9},{11,1... | collective-permute-start | bytes 442376 | tf_op jit(solution)/shard_map/ppermute | solution.py:365
  37.8 8.9 %collective-permute-start.5 = (bf16[3,4,48,128]{3,2,1,0:T(8,128)(2,1)S(1)}, bf16[3,4,48,128]{3,2,1,0:T(8,128)(2,1)S(1)}, u32[]{:S(2)}, u32[]{:S(2)}) collective-permute-start(bf16[3,4,48,128]{3,2,1,0:T(8,128)(2,1)S(1)} %get-tuple-element.60), channel_id=1, source_target_pairs={{0,1},{1,2},{2,3},{3,4},{4,5},{5,6},{6,7},{7,8},{8,9},{9,10},{10,1... | collective-permute-start | bytes 442376 | tf_op jit(solution)/shard_map/ppermute | solution.py:364
  49.8 16.7 %collective-permute-start.8 = (bf16[2,3,4,64,128]{4,3,2,1,0:T(8,128)(2,1)S(1)}, bf16[2,3,4,64,128]{4,3,2,1,0:T(8,128)(2,1)S(1)}, u32[]{:S(2)}, u32[]{:S(2)}) collective-permute-start(bf16[2,3,4,64,128]{4,3,2,1,0:T(8,128)(2,1)S(1)} %get-tuple-element.45), channel_id=1, source_target_pairs={{0,1},{1,2},{2,3},{3,4},{4,5},{5,6},{6,7},{7,8},{8,9},{9,10},{10,1... | collective-permute-start | bytes 1179656 | tf_op jit(solution)/shard_map/ppermute | solution.py:364
  49.9 16.6 %collective-permute-start.9 = (bf16[2,3,4,64,128]{4,3,2,1,0:T(8,128)(2,1)S(1)}, bf16[2,3,4,64,128]{4,3,2,1,0:T(8,128)(2,1)S(1)}, u32[]{:S(2)}, u32[]{:S(2)}) collective-permute-start(bf16[2,3,4,64,128]{4,3,2,1,0:T(8,128)(2,1)S(1)} %get-tuple-element.46), channel_id=1, source_target_pairs={{1,0},{2,1},{3,2},{4,3},{5,4},{6,5},{7,6},{8,7},{9,8},{10,9},{11,1... | collective-permute-start | bytes 1179656 | tf_op jit(solution)/shard_map/ppermute | solution.py:365
  55.9 7.8 %collective-permute-start.11 = (bf16[3,4,48,128]{3,2,1,0:T(8,128)(2,1)S(1)}, bf16[3,4,48,128]{3,2,1,0:T(8,128)(2,1)S(1)}, u32[]{:S(2)}, u32[]{:S(2)}) collective-permute-start(bf16[3,4,48,128]{3,2,1,0:T(8,128)(2,1)S(1)} %get-tuple-element.57), channel_id=1, source_target_pairs={{1,0},{2,1},{3,2},{4,3},{5,4},{6,5},{7,6},{8,7},{9,8},{10,9},{11,1... | collective-permute-start | bytes 442376 | tf_op jit(solution)/shard_map/ppermute | solution.py:365
  57.7 8.8 %collective-permute-start.10 = (bf16[3,4,48,128]{3,2,1,0:T(8,128)(2,1)S(1)}, bf16[3,4,48,128]{3,2,1,0:T(8,128)(2,1)S(1)}, u32[]{:S(2)}, u32[]{:S(2)}) collective-permute-start(bf16[3,4,48,128]{3,2,1,0:T(8,128)(2,1)S(1)} %get-tuple-element.58), channel_id=1, source_target_pairs={{0,1},{1,2},{2,3},{3,4},{4,5},{5,6},{6,7},{7,8},{8,9},{9,10},{10,1... | collective-permute-start | bytes 442376 | tf_op jit(solution)/shard_map/ppermute | solution.py:364
  69.7 12.2 %collective-permute-start.12 = (bf16[2,3,4,64,128]{4,3,2,1,0:T(8,128)(2,1)S(1)}, bf16[2,3,4,64,128]{4,3,2,1,0:T(8,128)(2,1)S(1)}, u32[]{:S(2)}, u32[]{:S(2)}) collective-permute-start(bf16[2,3,4,64,128]{4,3,2,1,0:T(8,128)(2,1)S(1)} %get-tuple-element.50), channel_id=1, source_target_pairs={{0,1},{1,2},{2,3},{3,4},{4,5},{5,6},{6,7},{7,8},{8,9},{9,10},{10,1... | collective-permute-start | bytes 1179656 | tf_op jit(solution)/shard_map/ppermute | solution.py:364
  69.8 12.1 %collective-permute-start.13 = (bf16[2,3,4,64,128]{4,3,2,1,0:T(8,128)(2,1)S(1)}, bf16[2,3,4,64,128]{4,3,2,1,0:T(8,128)(2,1)S(1)}, u32[]{:S(2)}, u32[]{:S(2)}) collective-permute-start(bf16[2,3,4,64,128]{4,3,2,1,0:T(8,128)(2,1)S(1)} %get-tuple-element.51), channel_id=1, source_target_pairs={{1,0},{2,1},{3,2},{4,3},{5,4},{6,5},{7,6},{8,7},{9,8},{10,9},{11,1... | collective-permute-start | bytes 1179656 | tf_op jit(solution)/shard_map/ppermute | solution.py:365
  85.1 12.0 %collective-permute-start.14 = (bf16[2,3,4,64,128]{4,3,2,1,0:T(8,128)(2,1)S(1)}, bf16[2,3,4,64,128]{4,3,2,1,0:T(8,128)(2,1)S(1)}, u32[]{:S(2)}, u32[]{:S(2)}) collective-permute-start(bf16[2,3,4,64,128]{4,3,2,1,0:T(8,128)(2,1)S(1)} %get-tuple-element.55), channel_id=1, source_target_pairs={{0,1},{1,2},{2,3},{3,4},{4,5},{5,6},{6,7},{7,8},{8,9},{9,10},{10,1... | collective-permute-start | bytes 1179656 | tf_op jit(solution)/shard_map/ppermute | solution.py:364
  85.2 11.9 %collective-permute-start.15 = (bf16[2,3,4,64,128]{4,3,2,1,0:T(8,128)(2,1)S(1)}, bf16[2,3,4,64,128]{4,3,2,1,0:T(8,128)(2,1)S(1)}, u32[]{:S(2)}, u32[]{:S(2)}) collective-permute-start(bf16[2,3,4,64,128]{4,3,2,1,0:T(8,128)(2,1)S(1)} %get-tuple-element.56), channel_id=1, source_target_pairs={{1,0},{2,1},{3,2},{4,3},{5,4},{6,5},{7,6},{8,7},{9,8},{10,9},{11,1... | collective-permute-start | bytes 1179656 | tf_op jit(solution)/shard_map/ppermute | solution.py:365
  91.1 6.0 %copy-start.4 = (bf16[512,512]{1,0:T(8,128)(2,1)S(1)}, bf16[512,512]{1,0:T(8,128)(2,1)}, u32[]{:S(2)}) copy-start(bf16[512,512]{1,0:T(8,128)(2,1)} %constant.5.clone.refs_16_) | copy-start | bytes 1572868

commit v3 on v2

--- a/solution.py
+++ b/solution.py
@@ -15,11 +15,12 @@
 WIDE = 6
 RIM = WIDE * LEV
 NEAR = 2 * LEV
-RUN = 4
+RUN = (7, 14, 12, 10)
 SIDE = 16 * LEV
 HANDED = (((2, 8), (26, 4)), ((4, 10), (24, 2)))
 INTERIOR_FLOPS = 1_000_000
 VMEM_LIMIT = 34 * 1024 * 1024
+BASE_VMEM_LIMIT = 61 * 1024 * 1024
 F32, BF16 = jnp.float32, jnp.bfloat16
 
 
@@ -84,29 +85,43 @@
     return (first, 1 - first), which
 
 
-def base_kernel(table_ref, traj_ref, order_ref, core_a, core_b, head_ref, tail_ref, rows):
+def base_kernel(table_ref, traj_ref, core_a, core_b, head_ref, tail_ref, slots, order_ref, rows, sems):
     turns, _ = timetable(table_ref, traj_ref.shape[0])
+    copies = [
+        pltpu.make_async_copy(traj_ref.at[turns[turn]], slots.at[turn], sems.at[turn]) for turn in range(2)
+    ]
+    for copy in copies:
+        copy.start()
+    lat = lax.broadcasted_iota(jnp.int32, (NLAT, NLAT), 0)
+    place = lax.broadcasted_iota(jnp.int32, (NLAT, NLAT), 1)
+    order_ref[...] = jnp.where((lat & (NK - 1)) * LANES + (lat >> 2) == place, 1.0, 0.0).astype(BF16)
     for turn, core_ref in enumerate((core_a, core_b)):
+        copies[turn].wait()
         for c in range(3):
-            scatter_rows(dot(traj_ref[turns[turn], c].reshape(LEV * LON, NLAT), order_ref[...]), rows.at[c])
+            scatter_rows(dot(slots[turn, c].reshape(LEV * LON, NLAT), order_ref[...]), rows.at[c])
             for k in range(NK):
                 core_ref[c, k] = rows[c, k].astype(BF16)
                 head_ref[turn, c, k] = rows[c, k, pl.ds(0, RIM), :].astype(BF16)
                 tail_ref[turn, c, k] = rows[c, k, pl.ds(CORE - RIM, RIM), :].astype(BF16)
 
 
-def convert_base(table, trajectory, order):
+def convert_base(table, trajectory):
     return pl.pallas_call(
         base_kernel,
-        in_specs=[pl.BlockSpec(memory_space=pltpu.SMEM)] + [pl.BlockSpec(memory_space=pltpu.VMEM)] * 2,
+        in_specs=[pl.BlockSpec(memory_space=pltpu.SMEM), pl.BlockSpec(memory_space=pl.ANY)],
         out_specs=[pl.BlockSpec(memory_space=pltpu.VMEM)] * 4,
         out_shape=[jax.ShapeDtypeStruct((3, NK, CORE, LANES), BF16)] * 2
         + [jax.ShapeDtypeStruct((2, 3, NK, RIM, LANES), BF16)] * 2,
-        scratch_shapes=[pltpu.VMEM((3, NK, CORE, LANES), F32)],
-        compiler_params=pltpu.CompilerParams(vmem_limit_bytes=VMEM_LIMIT),
+        scratch_shapes=[
+            pltpu.VMEM((2, 3, LEV, LON, NLAT), BF16),
+            pltpu.VMEM((NLAT, NLAT), BF16),
+            pltpu.VMEM((3, NK, CORE, LANES), F32),
+            pltpu.SemaphoreType.DMA((2,)),
+        ],
+        compiler_params=pltpu.CompilerParams(vmem_limit_bytes=BASE_VMEM_LIMIT),
         cost_estimate=pl.CostEstimate(flops=1_000_000, bytes_accessed=100_000, transcendentals=0),
         name="convert_base",
-    )(table, trajectory, order)
+    )(table, trajectory)
 
 
 def vectors_kernel(vec_ref, order_ref, core_ref, head_ref, tail_ref):
@@ -229,14 +244,14 @@
                 for k in range(NK):
                     base[c, k] = core[c, k].astype(F32)
 
-    sweep(2 * LEV, 30 * LEV, RUN, lambda row: derive(base, der, row, RUN))
+    sweep(2 * LEV, 30 * LEV, RUN[0], lambda row: derive(base, der, row, RUN[0]))
 
     def vector(v, carry):
         one = p_ref.at[v]
         last = into(out_ref.at[v])
-        sweep(2 * LEV, 30 * LEV, RUN, lambda row: stage(one, one, der, row, RUN, 0.0, 1.0, into(two)))
-        sweep(4 * LEV, 28 * LEV, RUN, lambda row: stage(two, one, der, row, RUN, 3.0, 1.0, into(three)))
-        sweep(6 * LEV, 26 * LEV, RUN, lambda row: stage(three, one, der, row, RUN, 2.0, 1.0 / 6.0, last))
+        sweep(2 * LEV, 30 * LEV, RUN[1], lambda row: stage(one, one, der, row, RUN[1], 0.0, 1.0, into(two)))
+        sweep(4 * LEV, 28 * LEV, RUN[2], lambda row: stage(two, one, der, row, RUN[2], 3.0, 1.0, into(three)))
+        sweep(6 * LEV, 26 * LEV, RUN[3], lambda row: stage(three, one, der, row, RUN[3], 2.0, 1.0 / 6.0, last))
         for c in range(3):
             for k in range(NK):
                 for i, (held, places) in enumerate(zip((two, three), HANDED)):
@@ -369,7 +384,7 @@
 def on_device(order, order_back, vectors, trajectory, slot_table):
     slots = trajectory.shape[0]
     swap = [(0, 1), (1, 0)]
-    own_a, own_b, head, tail = convert_base(slot_table, trajectory, order)
+    own_a, own_b, head, tail = convert_base(slot_table, trajectory)
     got = [lax.ppermute(core, "member", swap) for core in (own_a, own_b)]
     own = (own_a, own_b, *neighbours(head, tail))
 

time: 104 us -> 103 us (level)
  local copies, waits for them, and re-layouts: 6.08 us -> 2.99 us
  waiting for transfers between devices: 19.1 us -> 20.2 us
    unnamed x14 -> x12, local copies, waits for them, and re-layouts: 6.04 us -> 2.95 us
    pallas_call x1, Pallas kernels: 1.94 us -> 4.57 us  [convert_base(): pl.pallas_call(base_kernel, in_specs=[pl.BlockSpec(memory_space=pltpu.SME...]
    pallas_call x4, Pallas kernels: 24.1 us -> 22.1 us  [interior(): pl.pallas_call(functools.partial(interior_kernel, step, slots), in_specs=...]
  transfers between devices with their start and end apart: 16 -> 16, of which waited for: 3 -> 3; matrix products, arithmetic and copies ran while one was open for 0% -> 0% of each run, Pallas kernels for 29% -> 28%
where the time goes in v3:
time: 103 us
  Pallas kernels  46.2 us (45%)
  starting transfers between devices  33.1 us (32%)
  waiting for transfers between devices  20.2 us (20%)
  local copies, waits for them, and re-layouts  2.99 us (3%)
    ppermute x7, starting transfers between devices, neighbours(): lax.ppermute(head, 'tile', [((i + 1) % count, i) for i in range(count)])  29.2 us
    pallas_call x4, Pallas kernels, interior(): pl.pallas_call(functools.partial(interior_kernel, step, slots), in_specs=...  22.1 us
    pallas_call x4, Pallas kernels, boundary(): pl.pallas_call(functools.partial(boundary_kernel, step, slots, last), in_...  16.4 us
    ppermute x2, waiting for transfers between devices, on_device(): got = [lax.ppermute(core, 'member', swap) for core in (own_a, own_b)]  13.6 us
    ppermute x7, waiting for transfers between devices, neighbours(): lax.ppermute(tail, 'tile', [(i, (i + 1) % count) for i in range(count)])  6.59 us
    pallas_call x1, Pallas kernels, convert_base(): pl.pallas_call(base_kernel, in_specs=[pl.BlockSpec(memory_space=pltpu.SME...  4.57 us
    ppermute x2, starting transfers between devices, on_device(): got = [lax.ppermute(core, 'member', swap) for core in (own_a, own_b)]  3.61 us
    pallas_call x1, Pallas kernels, convert_vectors(): pl.pallas_call(vectors_kernel, grid=(nv, 3), in_specs=[pl.BlockSpec((1, 1...  3.19 us
  transfers between devices with their start and end apart: 16, of which 3 were waited for; matrix products, arithmetic and copies ran while one was open for 0% of the time, Pallas kernels for 28%

profile of v3, /device:TPU:0, one launch (start us, length us, event | category | flops | bytes accessed | tf_op | source)
XLA Modules:
  0.0 102.7 jit_solution(1796400476474171166)
XLA Ops:
  0.0 4.6 %convert_base.1 = (bf16[3,4,256,128]{3,2,1,0:T(8,128)(2,1)}, bf16[3,4,256,128]{3,2,1,0:T(8,128)(2,1)}, bf16[2,3,4,48,128]{4,3,2,1,0:T(8,128)(2,1)}, bf16[2,3,4,48,128]{4,3,2,1,0:T(8,128)(2,1)}) custom-call(s32[4]{0:T(128)} %refs_0_.7, bf16[2,3,8,32,512]{4,3,2,1,0:T(8,128)(2,1)} %traj_ref.1), custom_call_target="tpu_custom_call" | custom-call | flops 1000000 | bytes 100000 | tf_op jit(solution)/shard_map/convert_base/pallas_call | solution.py:109
  4.6 0.0 copy-start
  4.6 3.3 %collective-permute-start = (bf16[3,4,256,128]{3,2,1,0:T(8,128)(2,1)}, bf16[3,4,256,128]{3,2,1,0:T(8,128)(2,1)S(1)}, u32[]{:S(2)}, u32[]{:S(2)}) collective-permute-start(bf16[3,4,256,128]{3,2,1,0:T(8,128)(2,1)} %get-tuple-element.32.refs_0_.refs_6_), channel_id=1, source_target_pairs={{0,64},{64,0},{1,65},{65,1},{2,66},{66,2},{3,67},{67,3},{4,68},{68... | collective-permute-start | bytes 2359304 | tf_op jit(solution)/shard_map/ppermute | solution.py:388
  7.9 0.3 collective-permute-start.7
  8.2 0.0 collective-permute-start.3
  8.2 6.2 %collective-permute-start.4 = (bf16[2,3,4,48,128]{4,3,2,1,0:T(8,128)(2,1)}, bf16[2,3,4,48,128]{4,3,2,1,0:T(8,128)(2,1)S(1)}, u32[]{:S(2)}, u32[]{:S(2)}) collective-permute-start(bf16[2,3,4,48,128]{4,3,2,1,0:T(8,128)(2,1)} %get-tuple-element.39), channel_id=1, source_target_pairs={{1,0},{2,1},{3,2},{4,3},{5,4},{6,5},{7,6},{8,7},{9,8},{10,9},{11,1... | collective-permute-start | bytes 884744 | tf_op jit(solution)/shard_map/ppermute | solution.py:380
  14.4 1.9 %copy-done.2 = f32[2,3,8,32,512]{4,3,2,1,0:T(8,128)S(1)} copy-done((f32[2,3,8,32,512]{4,3,2,1,0:T(8,128)S(1)}, f32[2,3,8,32,512]{4,3,2,1,0:T(8,128)}, u32[]{:S(2)}) %copy-start.2) | copy-done | bytes 3145752
  16.3 1.0 %copy-done.4 = bf16[512,512]{1,0:T(8,128)(2,1)S(1)} copy-done((bf16[512,512]{1,0:T(8,128)(2,1)S(1)}, bf16[512,512]{1,0:T(8,128)(2,1)}, u32[]{:S(2)}) %copy-start.4) | copy-done | bytes 524312
  17.3 3.2 %convert_vectors.1 = (f32[2,3,4,256,128]{4,3,2,1,0:T(8,128)S(1)}, bf16[2,3,4,64,128]{4,3,2,1,0:T(8,128)(2,1)S(1)}, bf16[2,3,4,64,128]{4,3,2,1,0:T(8,128)(2,1)S(1)}) custom-call(f32[2,3,8,32,512]{4,3,2,1,0:T(8,128)S(1)} %copy-done.2, bf16[512,512]{1,0:T(8,128)(2,1)S(1)} %copy-done.4), custom_call_target="tpu_custom_call" | custom-call | flops 1000000 | bytes 100000 | tf_op jit(solution)/shard_map/convert_vectors/pallas_call | solution.py:135
  20.6 0.1 collective-permute-start.1
  20.6 13.6 %collective-permute-done.refs_1_.refs_10_.refs_2_ = bf16[3,4,256,128]{3,2,1,0:T(8,128)(2,1)S(1)} collective-permute-done((bf16[3,4,256,128]{3,2,1,0:T(8,128)(2,1)}, bf16[3,4,256,128]{3,2,1,0:T(8,128)(2,1)S(1)}, u32[]{:S(2)}, u32[]{:S(2)}) %collective-permute-start) | collective-permute-done | bytes 786464 | tf_op jit(solution)/shard_map/ppermute | solution.py:388
  34.2 0.5 collective-permute-start.2
  34.7 2.8 %collective-permute-start.6 = (bf16[3,4,48,128]{3,2,1,0:T(8,128)(2,1)S(1)}, bf16[3,4,48,128]{3,2,1,0:T(8,128)(2,1)S(1)}, u32[]{:S(2)}, u32[]{:S(2)}) collective-permute-start(bf16[3,4,48,128]{3,2,1,0:T(8,128)(2,1)S(1)} %get-tuple-element.59), channel_id=1, source_target_pairs={{1,0},{2,1},{3,2},{4,3},{5,4},{6,5},{7,6},{8,7},{9,8},{10,9},{11,1... | collective-permute-start | bytes 442376 | tf_op jit(solution)/shard_map/ppermute | solution.py:380
  37.5 0.0 collective-permute-done.4.refs_9_
  37.5 0.0 collective-permute-start.5
  37.6 5.5 %interior.4 = (f32[2,3,4,256,128]{4,3,2,1,0:T(8,128)S(1)}, f32[2,3,4,128,128]{4,3,2,1,0:T(8,128)S(1)}) custom-call(s32[4]{0:T(128)S(1)} %copy-done.5, f32[2,3,4,256,128]{4,3,2,1,0:T(8,128)S(1)} %get-tuple-element.31.p_ref.refs_1_, bf16[3,4,256,128]{3,2,1,0:T(8,128)(2,1)S(1)} %copy-done, bf16[3,4,256,128]{3,2,1,0:T(8,128)(2,1)S(1)} %collective-permute-done.refs_1_.refs_10_.refs_2_), custom_call_target="tpu_custom_call" | custom-call | flops 1000000 | bytes 100000 | tf_op jit(solution)/shard_map/interior/pallas_call | solution.py:269
  43.1 3.3 %collective-permute-done.5.refs_11_ = bf16[3,4,48,128]{3,2,1,0:T(8,128)(2,1)S(1)} collective-permute-done((bf16[3,4,48,128]{3,2,1,0:T(8,128)(2,1)S(1)}, bf16[3,4,48,128]{3,2,1,0:T(8,128)(2,1)S(1)}, u32[]{:S(2)}, u32[]{:S(2)}) %collective-permute-start.5) | collective-permute-done | bytes 147488 | tf_op jit(solution)/shard_map/ppermute | solution.py:379
  46.4 3.1 %boundary.3 = (f32[2,3,4,256,128]{4,3,2,1,0:T(8,128)S(1)}, bf16[2,3,4,64,128]{4,3,2,1,0:T(8,128)(2,1)S(1)}, bf16[2,3,4,64,128]{4,3,2,1,0:T(8,128)(2,1)S(1)}) custom-call(s32[4]{0:T(128)S(1)} %copy-done.5, f32[2,3,4,256,128]{4,3,2,1,0:T(8,128)S(1)} %get-tuple-element.31.p_ref.refs_1_, f32[2,3,4,256,128]{4,3,2,1,0:T(8,128)S(1)} %get-tuple-element.33.refs_2_, ...), custom_call_target="tpu_custom_call" | custom-call | flops 1000000 | bytes 100000 | tf_op jit(solution)/shard_map/boundary/pallas_call | solution.py:365
  49.6 0.1 collective-permute-start.8
  49.7 6.0 %collective-permute-start.9 = (bf16[2,3,4,64,128]{4,3,2,1,0:T(8,128)(2,1)S(1)}, bf16[2,3,4,64,128]{4,3,2,1,0:T(8,128)(2,1)S(1)}, u32[]{:S(2)}, u32[]{:S(2)}) collective-permute-start(bf16[2,3,4,64,128]{4,3,2,1,0:T(8,128)(2,1)S(1)} %get-tuple-element.46), channel_id=1, source_target_pairs={{1,0},{2,1},{3,2},{4,3},{5,4},{6,5},{7,6},{8,7},{9,8},{10,9},{11,1... | collective-permute-start | bytes 1179656 | tf_op jit(solution)/shard_map/ppermute | solution.py:380
  55.6 1.8 %collective-permute-start.11 = (bf16[3,4,48,128]{3,2,1,0:T(8,128)(2,1)S(1)}, bf16[3,4,48,128]{3,2,1,0:T(8,128)(2,1)S(1)}, u32[]{:S(2)}, u32[]{:S(2)}) collective-permute-start(bf16[3,4,48,128]{3,2,1,0:T(8,128)(2,1)S(1)} %get-tuple-element.57), channel_id=1, source_target_pairs={{1,0},{2,1},{3,2},{4,3},{5,4},{6,5},{7,6},{8,7},{9,8},{10,9},{11,1... | collective-permute-start | bytes 442376 | tf_op jit(solution)/shard_map/ppermute | solution.py:380
  57.5 5.5 %interior.5 = (f32[2,3,4,256,128]{4,3,2,1,0:T(8,128)S(1)}, f32[2,3,4,128,128]{4,3,2,1,0:T(8,128)S(1)}) custom-call(s32[4]{0:T(128)S(1)} %copy-done.5, f32[2,3,4,256,128]{4,3,2,1,0:T(8,128)S(1)} %get-tuple-element.41.p_ref.refs_1_, bf16[3,4,256,128]{3,2,1,0:T(8,128)(2,1)S(1)} %copy-done, bf16[3,4,256,128]{3,2,1,0:T(8,128)(2,1)S(1)} %copy-done.1, ...), custom_call_target="tpu_custom_call" | custom-call | flops 1000000 | bytes 100000 | tf_op jit(solution)/shard_map/interior/pallas_call | solution.py:269
  63.0 3.3 %collective-permute-done.10.refs_14_ = bf16[3,4,48,128]{3,2,1,0:T(8,128)(2,1)S(1)} collective-permute-done((bf16[3,4,48,128]{3,2,1,0:T(8,128)(2,1)S(1)}, bf16[3,4,48,128]{3,2,1,0:T(8,128)(2,1)S(1)}, u32[]{:S(2)}, u32[]{:S(2)}) %collective-permute-start.10) | collective-permute-done | bytes 147488 | tf_op jit(solution)/shard_map/ppermute | solution.py:379
  66.2 3.3 %boundary.4 = (f32[2,3,4,256,128]{4,3,2,1,0:T(8,128)S(1)}, bf16[2,3,4,64,128]{4,3,2,1,0:T(8,128)(2,1)S(1)}, bf16[2,3,4,64,128]{4,3,2,1,0:T(8,128)(2,1)S(1)}) custom-call(s32[4]{0:T(128)S(1)} %copy-done.5, f32[2,3,4,256,128]{4,3,2,1,0:T(8,128)S(1)} %get-tuple-element.41.p_ref.refs_1_, f32[2,3,4,256,128]{4,3,2,1,0:T(8,128)S(1)} %get-tuple-element.43.refs_2_, ...), custom_call_target="tpu_custom_call" | custom-call | flops 1000000 | bytes 100000 | tf_op jit(solution)/shard_map/boundary/pallas_call | solution.py:365
  69.6 0.1 collective-permute-start.12
  69.7 6.0 %collective-permute-start.13 = (bf16[2,3,4,64,128]{4,3,2,1,0:T(8,128)(2,1)S(1)}, bf16[2,3,4,64,128]{4,3,2,1,0:T(8,128)(2,1)S(1)}, u32[]{:S(2)}, u32[]{:S(2)}) collective-permute-start(bf16[2,3,4,64,128]{4,3,2,1,0:T(8,128)(2,1)S(1)} %get-tuple-element.51), channel_id=1, source_target_pairs={{1,0},{2,1},{3,2},{4,3},{5,4},{6,5},{7,6},{8,7},{9,8},{10,9},{11,1... | collective-permute-start | bytes 1179656 | tf_op jit(solution)/shard_map/ppermute | solution.py:380
  75.6 5.5 %interior.6 = (f32[2,3,4,256,128]{4,3,2,1,0:T(8,128)S(1)}, f32[2,3,4,128,128]{4,3,2,1,0:T(8,128)S(1)}) custom-call(s32[4]{0:T(128)S(1)} %copy-done.5, f32[2,3,4,256,128]{4,3,2,1,0:T(8,128)S(1)} %get-tuple-element.47.p_ref.refs_1_, bf16[3,4,256,128]{3,2,1,0:T(8,128)(2,1)S(1)} %copy-done, bf16[3,4,256,128]{3,2,1,0:T(8,128)(2,1)S(1)} %copy-done.1, ...), custom_call_target="tpu_custom_call" | custom-call | flops 1000000 | bytes 100000 | tf_op jit(solution)/shard_map/interior/pallas_call | solution.py:269
  81.2 3.2 %boundary.5 = (f32[2,3,4,256,128]{4,3,2,1,0:T(8,128)S(1)}, bf16[2,3,4,64,128]{4,3,2,1,0:T(8,128)(2,1)S(1)}, bf16[2,3,4,64,128]{4,3,2,1,0:T(8,128)(2,1)S(1)}) custom-call(s32[4]{0:T(128)S(1)} %copy-done.5, f32[2,3,4,256,128]{4,3,2,1,0:T(8,128)S(1)} %get-tuple-element.47.p_ref.refs_1_, f32[2,3,4,256,128]{4,3,2,1,0:T(8,128)S(1)} %get-tuple-element.48.refs_2_, ...), custom_call_target="tpu_custom_call" | custom-call | flops 1000000 | bytes 100000 | tf_op jit(solution)/shard_map/boundary/pallas_call | solution.py:365
  84.3 0.1 collective-permute-start.14
  84.4 6.0 %collective-permute-start.15 = (bf16[2,3,4,64,128]{4,3,2,1,0:T(8,128)(2,1)S(1)}, bf16[2,3,4,64,128]{4,3,2,1,0:T(8,128)(2,1)S(1)}, u32[]{:S(2)}, u32[]{:S(2)}) collective-permute-start(bf16[2,3,4,64,128]{4,3,2,1,0:T(8,128)(2,1)S(1)} %get-tuple-element.56), channel_id=1, source_target_pairs={{1,0},{2,1},{3,2},{4,3},{5,4},{6,5},{7,6},{8,7},{9,8},{10,9},{11,1... | collective-permute-start | bytes 1179656 | tf_op jit(solution)/shard_map/ppermute | solution.py:380
  90.4 5.5 %interior.7 = (f32[2,3,4,256,128]{4,3,2,1,0:T(8,128)S(1)}, f32[2,3,4,128,128]{4,3,2,1,0:T(8,128)S(1)}) custom-call(s32[4]{0:T(128)S(1)} %copy-done.5, f32[2,3,4,256,128]{4,3,2,1,0:T(8,128)S(1)} %get-tuple-element.52.p_ref.refs_1_, bf16[3,4,256,128]{3,2,1,0:T(8,128)(2,1)S(1)} %copy-done, bf16[3,4,256,128]{3,2,1,0:T(8,128)(2,1)S(1)} %copy-done.1, ...), custom_call_target="tpu_custom_call" | custom-call | flops 1000000 | bytes 100000 | tf_op jit(solution)/shard_map/interior/pallas_call | solution.py:269
  95.9 6.8 %last_boundary.1 = f32[2,3,8,32,512]{4,3,2,1,0:T(8,128)} custom-call(s32[4]{0:T(128)S(1)} %copy-done.5, f32[2,3,4,256,128]{4,3,2,1,0:T(8,128)S(1)} %get-tuple-element.52.p_ref.refs_1_, f32[2,3,4,256,128]{4,3,2,1,0:T(8,128)S(1)} %get-tuple-element.53.refs_2_, f32[2,3,4,128,128]{4,3,2,1,0:T(8,128)S(1)} %get-tuple-element.54.refs_3_, ...), custom_call_target="tpu_custom_call" | custom-call | flops 1000000 | bytes 100000 | tf_op jit(solution)/shard_map/last_boundary/pallas_call | solution.py:365
  (24 shorter events, 0.1 us)
Async XLA Ops:
  0.0 37.5 %copy-start.5 = (s32[4]{0:T(128)S(1)}, s32[4]{0:T(128)}, u32[]{:S(2)}) copy-start(s32[4]{0:T(128)} %refs_0_.7) | copy-start | bytes 52
  4.6 33.0 %copy-start = (bf16[3,4,256,128]{3,2,1,0:T(8,128)(2,1)S(1)}, bf16[3,4,256,128]{3,2,1,0:T(8,128)(2,1)}, u32[]{:S(2)}) copy-start(bf16[3,4,256,128]{3,2,1,0:T(8,128)(2,1)} %get-tuple-element.32.refs_0_.refs_6_) | copy-start | bytes 2359300
  4.6 29.6 %collective-permute-start = (bf16[3,4,256,128]{3,2,1,0:T(8,128)(2,1)}, bf16[3,4,256,128]{3,2,1,0:T(8,128)(2,1)S(1)}, u32[]{:S(2)}, u32[]{:S(2)}) collective-permute-start(bf16[3,4,256,128]{3,2,1,0:T(8,128)(2,1)} %get-tuple-element.32.refs_0_.refs_6_), channel_id=1, source_target_pairs={{0,64},{64,0},{1,65},{65,1},{2,66},{66,2},{3,67},{67,3},{4,68},{68... | collective-permute-start | bytes 2359304 | tf_op jit(solution)/shard_map/ppermute | solution.py:388
  7.9 47.7 %collective-permute-start.7 = (bf16[3,4,256,128]{3,2,1,0:T(8,128)(2,1)}, bf16[3,4,256,128]{3,2,1,0:T(8,128)(2,1)S(1)}, u32[]{:S(2)}, u32[]{:S(2)}) collective-permute-start(bf16[3,4,256,128]{3,2,1,0:T(8,128)(2,1)} %get-tuple-element.37.refs_7_.refs_1_), channel_id=1, source_target_pairs={{0,64},{64,0},{1,65},{65,1},{2,66},{66,2},{3,67},{67,3},{4,68},{68... | collective-permute-start | bytes 2359304 | tf_op jit(solution)/shard_map/ppermute | solution.py:388
  8.2 26.5 %collective-permute-start.3 = (bf16[2,3,4,48,128]{4,3,2,1,0:T(8,128)(2,1)}, bf16[2,3,4,48,128]{4,3,2,1,0:T(8,128)(2,1)S(1)}, u32[]{:S(2)}, u32[]{:S(2)}) collective-permute-start(bf16[2,3,4,48,128]{4,3,2,1,0:T(8,128)(2,1)} %get-tuple-element.38), channel_id=1, source_target_pairs={{0,1},{1,2},{2,3},{3,4},{4,5},{5,6},{6,7},{7,8},{8,9},{9,10},{10,1... | collective-permute-start | bytes 884744 | tf_op jit(solution)/shard_map/ppermute | solution.py:379
  8.2 29.3 %collective-permute-start.4 = (bf16[2,3,4,48,128]{4,3,2,1,0:T(8,128)(2,1)}, bf16[2,3,4,48,128]{4,3,2,1,0:T(8,128)(2,1)S(1)}, u32[]{:S(2)}, u32[]{:S(2)}) collective-permute-start(bf16[2,3,4,48,128]{4,3,2,1,0:T(8,128)(2,1)} %get-tuple-element.39), channel_id=1, source_target_pairs={{1,0},{2,1},{3,2},{4,3},{5,4},{6,5},{7,6},{8,7},{9,8},{10,9},{11,1... | collective-permute-start | bytes 884744 | tf_op jit(solution)/shard_map/ppermute | solution.py:380
  14.4 1.9 %copy-start.2 = (f32[2,3,8,32,512]{4,3,2,1,0:T(8,128)S(1)}, f32[2,3,8,32,512]{4,3,2,1,0:T(8,128)}, u32[]{:S(2)}) copy-start(f32[2,3,8,32,512]{4,3,2,1,0:T(8,128)} %vec_ref.1) | copy-start | bytes 9437188
  16.3 1.0 %copy-start.4 = (bf16[512,512]{1,0:T(8,128)(2,1)S(1)}, bf16[512,512]{1,0:T(8,128)(2,1)}, u32[]{:S(2)}) copy-start(bf16[512,512]{1,0:T(8,128)(2,1)} %constant.4.clone.order_ref) | copy-start | bytes 1572868
  20.5 25.9 %copy-start.1 = (bf16[3,4,256,128]{3,2,1,0:T(8,128)(2,1)S(1)}, bf16[3,4,256,128]{3,2,1,0:T(8,128)(2,1)}, u32[]{:S(2)}) copy-start(bf16[3,4,256,128]{3,2,1,0:T(8,128)(2,1)} %get-tuple-element.37.refs_7_.refs_1_) | copy-start | bytes 2359300
  20.6 22.5 %collective-permute-start.1 = (bf16[2,3,4,64,128]{4,3,2,1,0:T(8,128)(2,1)S(1)}, bf16[2,3,4,64,128]{4,3,2,1,0:T(8,128)(2,1)S(1)}, u32[]{:S(2)}, u32[]{:S(2)}) collective-permute-start(bf16[2,3,4,64,128]{4,3,2,1,0:T(8,128)(2,1)S(1)} %get-tuple-element.35), channel_id=1, source_target_pairs={{0,1},{1,2},{2,3},{3,4},{4,5},{5,6},{6,7},{7,8},{8,9},{9,10},{10,1... | collective-permute-start | bytes 1179656 | tf_op jit(solution)/shard_map/ppermute | solution.py:379
  34.2 8.9 %collective-permute-start.2 = (bf16[2,3,4,64,128]{4,3,2,1,0:T(8,128)(2,1)S(1)}, bf16[2,3,4,64,128]{4,3,2,1,0:T(8,128)(2,1)S(1)}, u32[]{:S(2)}, u32[]{:S(2)}) collective-permute-start(bf16[2,3,4,64,128]{4,3,2,1,0:T(8,128)(2,1)S(1)} %get-tuple-element.36), channel_id=1, source_target_pairs={{1,0},{2,1},{3,2},{4,3},{5,4},{6,5},{7,6},{8,7},{9,8},{10,9},{11,1... | collective-permute-start | bytes 1179656 | tf_op jit(solution)/shard_map/ppermute | solution.py:380
  34.7 8.3 %collective-permute-start.6 = (bf16[3,4,48,128]{3,2,1,0:T(8,128)(2,1)S(1)}, bf16[3,4,48,128]{3,2,1,0:T(8,128)(2,1)S(1)}, u32[]{:S(2)}, u32[]{:S(2)}) collective-permute-start(bf16[3,4,48,128]{3,2,1,0:T(8,128)(2,1)S(1)} %get-tuple-element.59), channel_id=1, source_target_pairs={{1,0},{2,1},{3,2},{4,3},{5,4},{6,5},{7,6},{8,7},{9,8},{10,9},{11,1... | collective-permute-start | bytes 442376 | tf_op jit(solution)/shard_map/ppermute | solution.py:380
  37.5 8.9 %collective-permute-start.5 = (bf16[3,4,48,128]{3,2,1,0:T(8,128)(2,1)S(1)}, bf16[3,4,48,128]{3,2,1,0:T(8,128)(2,1)S(1)}, u32[]{:S(2)}, u32[]{:S(2)}) collective-permute-start(bf16[3,4,48,128]{3,2,1,0:T(8,128)(2,1)S(1)} %get-tuple-element.60), channel_id=1, source_target_pairs={{0,1},{1,2},{2,3},{3,4},{4,5},{5,6},{6,7},{7,8},{8,9},{9,10},{10,1... | collective-permute-start | bytes 442376 | tf_op jit(solution)/shard_map/ppermute | solution.py:379
  49.6 16.7 %collective-permute-start.8 = (bf16[2,3,4,64,128]{4,3,2,1,0:T(8,128)(2,1)S(1)}, bf16[2,3,4,64,128]{4,3,2,1,0:T(8,128)(2,1)S(1)}, u32[]{:S(2)}, u32[]{:S(2)}) collective-permute-start(bf16[2,3,4,64,128]{4,3,2,1,0:T(8,128)(2,1)S(1)} %get-tuple-element.45), channel_id=1, source_target_pairs={{0,1},{1,2},{2,3},{3,4},{4,5},{5,6},{6,7},{7,8},{8,9},{9,10},{10,1... | collective-permute-start | bytes 1179656 | tf_op jit(solution)/shard_map/ppermute | solution.py:379
  49.7 16.6 %collective-permute-start.9 = (bf16[2,3,4,64,128]{4,3,2,1,0:T(8,128)(2,1)S(1)}, bf16[2,3,4,64,128]{4,3,2,1,0:T(8,128)(2,1)S(1)}, u32[]{:S(2)}, u32[]{:S(2)}) collective-permute-start(bf16[2,3,4,64,128]{4,3,2,1,0:T(8,128)(2,1)S(1)} %get-tuple-element.46), channel_id=1, source_target_pairs={{1,0},{2,1},{3,2},{4,3},{5,4},{6,5},{7,6},{8,7},{9,8},{10,9},{11,1... | collective-permute-start | bytes 1179656 | tf_op jit(solution)/shard_map/ppermute | solution.py:380
  55.6 7.3 %collective-permute-start.11 = (bf16[3,4,48,128]{3,2,1,0:T(8,128)(2,1)S(1)}, bf16[3,4,48,128]{3,2,1,0:T(8,128)(2,1)S(1)}, u32[]{:S(2)}, u32[]{:S(2)}) collective-permute-start(bf16[3,4,48,128]{3,2,1,0:T(8,128)(2,1)S(1)} %get-tuple-element.57), channel_id=1, source_target_pairs={{1,0},{2,1},{3,2},{4,3},{5,4},{6,5},{7,6},{8,7},{9,8},{10,9},{11,1... | collective-permute-start | bytes 442376 | tf_op jit(solution)/shard_map/ppermute | solution.py:380
  57.4 8.8 %collective-permute-start.10 = (bf16[3,4,48,128]{3,2,1,0:T(8,128)(2,1)S(1)}, bf16[3,4,48,128]{3,2,1,0:T(8,128)(2,1)S(1)}, u32[]{:S(2)}, u32[]{:S(2)}) collective-permute-start(bf16[3,4,48,128]{3,2,1,0:T(8,128)(2,1)S(1)} %get-tuple-element.58), channel_id=1, source_target_pairs={{0,1},{1,2},{2,3},{3,4},{4,5},{5,6},{6,7},{7,8},{8,9},{9,10},{10,1... | collective-permute-start | bytes 442376 | tf_op jit(solution)/shard_map/ppermute | solution.py:379
  69.6 11.6 %collective-permute-start.12 = (bf16[2,3,4,64,128]{4,3,2,1,0:T(8,128)(2,1)S(1)}, bf16[2,3,4,64,128]{4,3,2,1,0:T(8,128)(2,1)S(1)}, u32[]{:S(2)}, u32[]{:S(2)}) collective-permute-start(bf16[2,3,4,64,128]{4,3,2,1,0:T(8,128)(2,1)S(1)} %get-tuple-element.50), channel_id=1, source_target_pairs={{0,1},{1,2},{2,3},{3,4},{4,5},{5,6},{6,7},{7,8},{8,9},{9,10},{10,1... | collective-permute-start | bytes 1179656 | tf_op jit(solution)/shard_map/ppermute | solution.py:379
  69.7 11.5 %collective-permute-start.13 = (bf16[2,3,4,64,128]{4,3,2,1,0:T(8,128)(2,1)S(1)}, bf16[2,3,4,64,128]{4,3,2,1,0:T(8,128)(2,1)S(1)}, u32[]{:S(2)}, u32[]{:S(2)}) collective-permute-start(bf16[2,3,4,64,128]{4,3,2,1,0:T(8,128)(2,1)S(1)} %get-tuple-element.51), channel_id=1, source_target_pairs={{1,0},{2,1},{3,2},{4,3},{5,4},{6,5},{7,6},{8,7},{9,8},{10,9},{11,1... | collective-permute-start | bytes 1179656 | tf_op jit(solution)/shard_map/ppermute | solution.py:380
  84.3 11.6 %collective-permute-start.14 = (bf16[2,3,4,64,128]{4,3,2,1,0:T(8,128)(2,1)S(1)}, bf16[2,3,4,64,128]{4,3,2,1,0:T(8,128)(2,1)S(1)}, u32[]{:S(2)}, u32[]{:S(2)}) collective-permute-start(bf16[2,3,4,64,128]{4,3,2,1,0:T(8,128)(2,1)S(1)} %get-tuple-element.55), channel_id=1, source_target_pairs={{0,1},{1,2},{2,3},{3,4},{4,5},{5,6},{6,7},{7,8},{8,9},{9,10},{10,1... | collective-permute-start | bytes 1179656 | tf_op jit(solution)/shard_map/ppermute | solution.py:379
  84.4 11.5 %collective-permute-start.15 = (bf16[2,3,4,64,128]{4,3,2,1,0:T(8,128)(2,1)S(1)}, bf16[2,3,4,64,128]{4,3,2,1,0:T(8,128)(2,1)S(1)}, u32[]{:S(2)}, u32[]{:S(2)}) collective-permute-start(bf16[2,3,4,64,128]{4,3,2,1,0:T(8,128)(2,1)S(1)} %get-tuple-element.56), channel_id=1, source_target_pairs={{1,0},{2,1},{3,2},{4,3},{5,4},{6,5},{7,6},{8,7},{9,8},{10,9},{11,1... | collective-permute-start | bytes 1179656 | tf_op jit(solution)/shard_map/ppermute | solution.py:380
  90.4 5.6 %copy-start.3 = (bf16[512,512]{1,0:T(8,128)(2,1)S(1)}, bf16[512,512]{1,0:T(8,128)(2,1)}, u32[]{:S(2)}) copy-start(bf16[512,512]{1,0:T(8,128)(2,1)} %constant.5.clone.refs_16_) | copy-start | bytes 1572868
